TPU v7x, 512 devices: a whole 4x8x8 slice. The times are simulated.
512 devices in a mesh: slab: 64 (over z, x, core), batch: 8 (over y).
Axes of the slice: x: 4, y: 8, z: 8, core: 2. Of those that a mesh axis runs over, the one named last changes fastest.
Arguments:
- features: bfloat16 [8, 256, 512, 128], P('batch', 'slab'), may hold values from -6 to 6
- cotangent: bfloat16 [8, 256, 512, 128], P('batch', 'slab'), may hold values from -6 to 6
- coords: int32 [8, 256], P('batch', 'slab'), may hold values from 0 to 16, as said below
- orientation: int32 [8], P('batch'), may hold values from 0 to 7
- kernel: bfloat16 [27, 128, 128], replicated, may hold values from -0.109375 to 0.109375
Outputs:
- output: bfloat16 [8, 256, 512, 128], P('batch', 'slab')
- input_grad: bfloat16 [8, 256, 512, 128], P('batch', 'slab')
- kernel_grad: float32 [3456, 128], replicated
Inputs may be any that keep to these rules, and one draw needn't show every extreme that they name: `coords`: for each volume and slab, its 4 entries list distinct brick positions first and the value 4 * 4 for the empty slots after them; the numbers of listed bricks of slab s and of slab s + 32 of the same volume add up to 4; in every volume some slab lists 4 bricks.
All inputs are finite; a program needn't handle non-finite values.
Results may differ from a plain program's by a relative error of at most 0.001.
Values may be sent and summed in bfloat16 or wider, within the bound.
A program may use at most 128 MiB of HBM per device.

v0:
```python
import jax
import jax.numpy as jnp
from jax import lax
from jax.sharding import PartitionSpec as P

B = 8
G = 4


def padded_2(cells, sides, width):
    for axis, dim in sides:
        count = lax.axis_size(axis)
        ends = count - 1
        head = lax.slice_in_dim(cells, 0, width, axis=dim)
        tail = lax.slice_in_dim(cells, cells.shape[dim] - width, cells.shape[dim], axis=dim)
        cells = jnp.concatenate(
            [
                lax.ppermute(tail, axis, [(i, (i + 1) % count) for i in range(ends)]),
                cells,
                lax.ppermute(head, axis, [((i + 1) % count, i) for i in range(ends)]),
            ],
            axis=dim,
        )
    return cells


def tap_table(flip_code):
    tap_ids = jnp.arange(27, dtype=jnp.int32)
    tap_z = tap_ids // 9
    tap_y = tap_ids // 3 % 3
    tap_x = tap_ids % 3
    tap_x = jnp.where(flip_code % 2 == 1, 2 - tap_x, tap_x)
    tap_y = jnp.where(flip_code // 2 % 2 == 1, 2 - tap_y, tap_y)
    tap_z = jnp.where(flip_code // 4 % 2 == 1, 2 - tap_z, tap_z)
    return tap_z * 9 + tap_y * 3 + tap_x


def unfold(patches, mirrored):
    brick_side = patches.shape[1] - 2
    channels = patches.shape[-1]
    pieces = []
    for tap_z in range(3):
        for tap_y in range(3):
            for tap_x in range(3):
                if mirrored:
                    start_z, start_y, start_x = (2 - tap_z, 2 - tap_y, 2 - tap_x)
                else:
                    start_z, start_y, start_x = (tap_z, tap_y, tap_x)
                pieces.append(
                    patches[
                        :,
                        start_z : start_z + brick_side,
                        start_y : start_y + brick_side,
                        start_x : start_x + brick_side,
                        :,
                    ]
                )
    return jnp.concatenate(pieces, axis=-1).reshape(-1, 27 * channels)


def brick_pass(patches, row_mask, forward_flat, backward_flat):
    brick_side = patches.shape[2] - 2
    channels = patches.shape[-1]
    x_cols = unfold(patches[:, 0], False)
    g_cols = unfold(patches[:, 1], True)
    cell_mask = jnp.repeat(row_mask, brick_side**3)[:, None]
    centre = patches[:, 1, 1 : brick_side + 1, 1 : brick_side + 1, 1 : brick_side + 1, :].reshape(
        -1, channels
    )
    centre = jnp.where(cell_mask, centre, jnp.zeros((), jnp.bfloat16))
    out_y = jnp.dot(x_cols, forward_flat, preferred_element_type=jnp.float32).astype(jnp.bfloat16)
    out_dx = jnp.dot(g_cols, backward_flat, preferred_element_type=jnp.float32).astype(jnp.bfloat16)
    kernel_term = lax.dot_general(
        x_cols, centre, (((0,), (0,)), ((), ())), preferred_element_type=jnp.float32
    )
    return (out_y, out_dx, kernel_term)


def run_blocks(patches, row_mask, forward_flat, backward_flat):
    count_rows = patches.shape[0]
    block_rows = min(count_rows, 2)
    block_count = count_rows // block_rows
    channels = forward_flat.shape[-1]
    grouped = patches.reshape((block_count, block_rows) + patches.shape[1:])
    block_masks = row_mask.reshape(block_count, block_rows)

    def one_block(running, inputs):
        block_patch, block_mask = inputs
        out_y, out_dx, kernel_term = brick_pass(
            block_patch, block_mask, forward_flat, backward_flat
        )
        return (running + kernel_term, (out_y, out_dx))

    zero_grad = jnp.zeros((forward_flat.shape[0], channels), jnp.float32)
    summed, (out_y, out_dx) = lax.scan(one_block, zero_grad, (grouped, block_masks))
    return (
        out_y.reshape(count_rows, -1, channels),
        out_dx.reshape(count_rows, -1, channels),
        summed,
    )


def shards(features, cotangent, coords, orientation, kernel):
    channels = kernel.shape[-1]
    slots = features.shape[1]
    lend_rows = slots // 2
    positions = coords[0]
    active = positions < G * G
    source = jnp.stack([features[0], cotangent[0]]).reshape(2, slots, B, B, B, channels)
    source = jnp.where(active[None, :, None, None, None, None], source, jnp.zeros((), jnp.bfloat16))
    grid_ids = jnp.arange(G, dtype=jnp.int32)[:, None] * G + jnp.arange(G, dtype=jnp.int32)[None, :]
    placing = (positions[None, None, :] == grid_ids[:, :, None]).astype(jnp.bfloat16)
    dense_slab = jnp.einsum(
        "yxs,kszqrc->kzyqxrc", placing, source, preferred_element_type=jnp.float32
    )
    dense_slab = dense_slab.astype(jnp.bfloat16).reshape(2, B, G * B, G * B, channels)
    boundary = jnp.stack([dense_slab[:, 0], dense_slab[:, B - 1]])
    extended = padded_2(boundary, (("slab", 0),), 1)
    lower_plane = extended[0]
    upper_plane = extended[3]
    stacked = jnp.concatenate([lower_plane[:, None], dense_slab, upper_plane[:, None]], axis=1)
    padded = jnp.pad(stacked, ((0, 0), (0, 0), (1, 1), (1, 1), (0, 0)))
    clipped = jnp.minimum(positions, G * G - 1)

    def extract(pos_row, pos_col):
        return lax.dynamic_slice(
            padded, (0, 0, pos_row * B, pos_col * B, 0), (2, B + 2, B + 2, B + 2, channels)
        )

    patches = jax.vmap(extract)(clipped // G, clipped % G)
    chooser = tap_table(orientation[0])[:, None] == jnp.arange(27, dtype=jnp.int32)[None, :]
    effective = jnp.einsum(
        "tu,uio->tio", chooser.astype(jnp.bfloat16), kernel, preferred_element_type=jnp.float32
    ).astype(jnp.bfloat16)
    forward_flat = effective.reshape(27 * channels, channels)
    backward_flat = jnp.swapaxes(effective, 1, 2).reshape(27 * channels, channels)
    out_y, out_dx, local_grad = run_blocks(patches, active, forward_flat, backward_flat)
    slot_mask = active[:, None, None]
    out_y = jnp.where(slot_mask, out_y, jnp.zeros((), jnp.bfloat16))
    out_dx = jnp.where(slot_mask, out_dx, jnp.zeros((), jnp.bfloat16))
    grad_scale = float(lax.axis_size("slab") * lax.axis_size("batch") * lend_rows * B**3) ** (-0.5)
    unmirrored = jnp.einsum(
        "tu,tio->uio",
        chooser.astype(jnp.float32),
        local_grad.reshape(27, channels, channels),
        precision=lax.Precision.HIGHEST,
    )
    local_grad = (unmirrored * grad_scale).reshape(27 * channels, channels)
    kernel_grad = lax.psum(local_grad, ("slab", "batch"))
    return (out_y[None], out_dx[None], kernel_grad)


def solution(mesh):
    in_specs = (
        P("batch", "slab", None, None),
        P("batch", "slab", None, None),
        P("batch", "slab"),
        P("batch"),
        P(),
    )
    out_specs = (P("batch", "slab", None, None), P("batch", "slab", None, None), P())
    return jax.shard_map(shards, mesh=mesh, in_specs=in_specs, out_specs=out_specs, check_vma=False)
```

profile of v0, /device:TPU:1, one launch (start us, length us, event | category | flops | bytes accessed | tf_op | source)
XLA Modules:
  0.0 393.9 jit_solution(5660314282333281775)
XLA Ops:
  7.2 0.7 broadcast_compare_fusion
  8.0 1.3 pad_maximum_fusion
  9.3 3.1 convert_bitcast_fusion
  12.5 1.9 copy-done.1
  14.4 1.6 copy.29
  16.0 1.0 slice_bitcast_fusion.3
  17.1 4.5 %collective-permute-start = (bf16[1,2,32,32,128]{4,3,2,1,0:T(8,128)(2,1)}, bf16[1,2,32,32,128]{4,3,2,1,0:T(8,128)(2,1)}, u32[]{:S(2)}, u32[]{:S(2)}) collective-permute-start(bf16[1,2,32,32,128]{4,3,2,1,0:T(8,128)(2,1)} %get-tuple-element.121), channel_id=1, source_target_pairs={{0,8},{8,16},{16,24},{24,32},{32,40},{40,48},{48,56},{56,64},{64,7... | collective-permute-start | bytes 1572872 | tf_op jit(solution)/shard_map/ppermute | solution.py:18
  21.6 6.5 %collective-permute-start.1 = (bf16[1,2,32,32,128]{4,3,2,1,0:T(8,128)(2,1)}, bf16[1,2,32,32,128]{4,3,2,1,0:T(8,128)(2,1)}, u32[]{:S(2)}, u32[]{:S(2)}) collective-permute-start(bf16[1,2,32,32,128]{4,3,2,1,0:T(8,128)(2,1)} %get-tuple-element.122), channel_id=1, source_target_pairs={{8,0},{16,8},{24,16},{32,24},{40,32},{48,40},{56,48},{64,56},{72,6... | collective-permute-start | bytes 1572872 | tf_op jit(solution)/shard_map/ppermute | solution.py:20
  28.9 9.1 %copy.43 = bf16[2,8,4,8,4,8,128]{6,1,0,5,4,3,2:T(8,128)(2,1)} copy(bf16[2,8,4,8,4,8,128]{6,4,2,5,3,1,0:T(4,128)(2,1)} %copy-done.1) | data formatting | bytes 8388608 | tf_op jit(solution)/shard_map/reshape | solution.py:116
  38.1 0.7 lt.79
  38.8 0.7 convolution_convert_fusion.2
  39.5 1.0 copy-done.2
  40.8 2.6 copy.36
  43.4 2.2 copy.30
  45.6 2.2 copy.32
  47.8 13.0 %select_maximum_fusion = bf16[2,10,34,34,128]{4,1,0,3,2:T(8,128)(2,1)} fusion(bf16[2,1,32,32,128]{4,1,0,3,2:T(2,128)(2,1)S(1)} %copy.32, bf16[2,8,32,32,128]{4,1,0,3,2:T(8,128)(2,1)} %bitcast.119, bf16[2,1,32,32,128]{4,1,0,3,2:T(2,128)(2,1)S(1)} %copy.30), kind=kLoop, calls=%fused_computation.75 | loop fusion | flops 56227840 | bytes 11161600 | tf_op jit(solution)/shard_map/concatenate | solution.py:121
  60.9 6.4 %gather_fusion = bf16[4,2,10,10,10,128]{5,2,1,4,3,0:T(8,128)(2,1)} fusion(bf16[2,10,34,34,128]{4,1,0,3,2:T(8,128)(2,1)} %select_maximum_fusion, s32[4]{0:T(128)S(1)} %fusion.39), kind=kCustom, calls=%fused_computation | custom fusion | bytes 4096080 | tf_op jit(solution)/shard_map/vmap()/gather | solution.py:126
  67.2 32.7 %while.15 = (s32[]{:T(128)}, f32[3456,128]{1,0:T(8,128)S(1)}, bf16[2,1024,128]{2,1,0:T(8,128)(2,1)}, bf16[2,1024,128]{2,1,0:T(8,128)(2,1)}, bf16[2,2,2,10,10,10,...) while((s32[]{:T(128)}, f32[3456,128]{1,0:T(8,128)S(1)}, ...), condition=%wide.region_1.2_spmd.clone, body=%wide.region_0.1_spmd.clone.sunk | while | flops 2719186944 | bytes 74236176 | solution.py:95
  67.2 1.7 constant_dynamic-slice_fusion.2
  69.0 0.5 copy.59
  76.4 2.0 fusion.62
  78.5 2.1 fusion.61
  80.6 2.8 convolution_add_fusion.2
  83.5 1.7 constant_dynamic-slice_fusion.2
  92.7 2.0 fusion.62
  94.8 2.1 fusion.61
  96.8 2.8 convolution_add_fusion.2
  100.0 2.3 fusion.12
  102.3 2.2 copy.39
  104.5 2.2 broadcast_select_fusion
  106.7 277.5 %all-reduce.3.cloned.1.call-done = f32[3456,128]{1,0:T(8,128)} async-done(((f32[3456,128]{1,0:T(8,128)}), f32[3456,128]{1,0:T(8,128)}) %all-reduce.3.cloned.1.call-update) | async-done | bytes 1769488 | tf_op jit(solution)/shard_map/psum | solution.py:149
  384.2 2.8 copy.128
  (156 shorter events, 14.3 us)
Async XLA Ops:
  7.2 31.6 %copy-start = (bf16[27,128,128]{2,1,0:T(8,128)(2,1)S(1)}, bf16[27,128,128]{2,1,0:T(8,128)(2,1)}, u32[]{:S(2)}) copy-start(bf16[27,128,128]{2,1,0:T(8,128)(2,1)} %param.11) | copy-start | bytes 2654212
  7.2 377.0 %all-reduce.3.cloned.1.call-start = ((), (), s32[]{:S(2)}) async-start(), calls=%async_computation | async-start | bytes 3538944 | tf_op jit(solution)/shard_map/psum | solution.py:149
  9.3 19.5 %copy-start.9 = (s32[1,4]{1,0:T(1,128)S(1)}, s32[1,4]{1,0:T(1,128)}, u32[]{:S(2)}) copy-start(s32[1,4]{1,0:T(1,128)} %param.9) | copy-start | bytes 52
  12.4 2.0 copy-start.1
  17.1 26.3 %collective-permute-start = (bf16[1,2,32,32,128]{4,3,2,1,0:T(8,128)(2,1)}, bf16[1,2,32,32,128]{4,3,2,1,0:T(8,128)(2,1)}, u32[]{:S(2)}, u32[]{:S(2)}) collective-permute-start(bf16[1,2,32,32,128]{4,3,2,1,0:T(8,128)(2,1)} %get-tuple-element.121), channel_id=1, source_target_pairs={{0,8},{8,16},{16,24},{24,32},{32,40},{40,48},{48,56},{56,64},{64,7... | collective-permute-start | bytes 1572872 | tf_op jit(solution)/shard_map/ppermute | solution.py:18
  21.6 24.0 %collective-permute-start.1 = (bf16[1,2,32,32,128]{4,3,2,1,0:T(8,128)(2,1)}, bf16[1,2,32,32,128]{4,3,2,1,0:T(8,128)(2,1)}, u32[]{:S(2)}, u32[]{:S(2)}) collective-permute-start(bf16[1,2,32,32,128]{4,3,2,1,0:T(8,128)(2,1)} %get-tuple-element.122), channel_id=1, source_target_pairs={{8,0},{16,8},{24,16},{32,24},{40,32},{48,40},{56,48},{64,56},{72,6... | collective-permute-start | bytes 1572872 | tf_op jit(solution)/shard_map/ppermute | solution.py:20
  39.5 1.0 copy-start.2
  47.8 19.4 %copy-start.10 = (pred[2,2]{1,0:T(4,128)(4,1)S(1)}, pred[2,2]{1,0:T(4,128)(4,1)}, u32[]{:S(2)}) copy-start(pred[2,2]{1,0:T(4,128)(4,1)} %lt.79) | copy-start | bytes 16
  73.1 3.3 copy-start.3
  73.1 3.3 copy-start.4
  75.5 3.0 copy-start.7
  78.5 4.9 %copy-start.5 = (bf16[2,1024,128]{2,1,0:T(8,128)(2,1)}, bf16[2,1024,128]{2,1,0:T(8,128)(2,1)S(1)}, u32[]{:S(2)}) copy-start(bf16[2,1024,128]{2,1,0:T(8,128)(2,1)S(1)} %fusion.62) | copy-start | bytes 1572868 | tf_op jit(solution)/shard_map/while
  80.6 2.9 copy-start.8
  89.4 3.3 copy-start.3
  89.4 3.3 copy-start.4
  91.7 3.0 copy-start.7
  94.8 4.9 %copy-start.5 = (bf16[2,1024,128]{2,1,0:T(8,128)(2,1)}, bf16[2,1024,128]{2,1,0:T(8,128)(2,1)S(1)}, u32[]{:S(2)}) copy-start(bf16[2,1024,128]{2,1,0:T(8,128)(2,1)S(1)} %fusion.62) | copy-start | bytes 1572868 | tf_op jit(solution)/shard_map/while
  96.8 2.9 copy-start.8
  100.0 4.6 %copy-start.6 = (bf16[2,1024,128]{2,1,0:T(8,128)(2,1)S(1)}, bf16[2,1024,128]{2,1,0:T(8,128)(2,1)}, u32[]{:S(2)}) copy-start(bf16[2,1024,128]{2,1,0:T(8,128)(2,1)} %get-tuple-element.48) | copy-start | bytes 1572868
Sparse Core Ops, SparseCore 0:
  104.7 279.5 all-reduce.2
where the time goes:
time: 394 us
  waiting for transfers between devices  278 us (71%)
  local copies, waits for them, and re-layouts  51.6 us (13%)
  matrix products  19.9 us (5%)
  other arithmetic  17.5 us (4%)
  between operations  15 us (4%)
  starting transfers between devices  11.1 us (3%)
    psum x1, waiting for transfers between devices, shards(): kernel_grad = lax.psum(local_grad, ('slab', 'batch'))  278 us
    concatenate x1, other arithmetic, shards(): jnp.concatenate([lower_plane[:, None], dense_slab, upper_plane[:, None]],...  13 us
    while x124, local copies, waits for them, and re-layouts  12.1 us
    reshape x1, local copies, waits for them, and re-layouts, shards(): dense_slab.astype(jnp.bfloat16).reshape(2, B, G * B, G * B, channels)  9.14 us
  transfers between devices with their start and end apart: 3, of which 1 were waited for; matrix products, arithmetic and copies ran while one was open for 5% of the time, Pallas kernels for 0%

commit v1 on v0

v1 whole, which is shorter than its diff:
```python
import functools

import jax
import jax.numpy as jnp
from jax import lax
from jax.experimental import pallas as pl
from jax.experimental.pallas import tpu as pltpu
from jax.sharding import PartitionSpec as P

C = 128
SLOTS = 4
CELLS = 512
TAPS = 27
NZ, NX, NY = 8, 4, 8
GROUP = 32
CHUNK = 28
QROWS = CHUNK * GROUP
BITS = 14.95
BF = jnp.bfloat16
F32 = jnp.float32
MESH = pl.DeviceIdType.MESH


def place():
    s = lax.axis_index("slab")
    return s // 8, lax.rem(s // 2, 4), lax.rem(s, 2), lax.axis_index("batch")


def device(z, x, core, y):
    return {"slab": z * 8 + x * 2 + core, "batch": y}


def remote(src, dst, send, recv, where):
    return pltpu.make_async_remote_copy(
        src_ref=src, dst_ref=dst, send_sem=send, recv_sem=recv, device_id=where, device_id_type=MESH
    )


def halo_kernel(feat, cot, coords, hv, hu, hc, send, recv):
    s = lax.axis_index("slab")
    up, down = lax.rem(s + 1, 64), lax.rem(s + 63, 64)
    barrier = pltpu.get_barrier_semaphore()
    for peer in (up, down):
        pl.semaphore_signal(barrier, inc=1, device_id={"slab": peer}, device_id_type=MESH)
    pl.semaphore_wait(barrier, 2)
    copies = []
    for d, (peer, plane) in enumerate(((up, 7), (down, 0))):
        for k, (src, dst) in enumerate(((feat.at[:, plane], hv), (cot.at[:, plane], hu), (coords, hc))):
            copies.append(remote(src, dst.at[d], send.at[d, k], recv.at[d, k], {"slab": peer}))
    for copy in copies:
        copy.start()
    for copy in copies:
        copy.wait()


def halo(feat, cot, coords):
    anywhere = pl.BlockSpec(memory_space=pl.ANY)
    return pl.pallas_call(
        halo_kernel,
        out_shape=[
            jax.ShapeDtypeStruct((2, SLOTS, 64, C), BF),
            jax.ShapeDtypeStruct((2, SLOTS, 64, C), BF),
            jax.ShapeDtypeStruct((2, 8, C), jnp.int32),
        ],
        in_specs=[anywhere] * 3,
        out_specs=[anywhere] * 3,
        scratch_shapes=[pltpu.SemaphoreType.DMA((2, 3)), pltpu.SemaphoreType.DMA((2, 3))],
        compiler_params=pltpu.CompilerParams(collective_id=0, has_side_effects=True),
        name="halo_planes",
    )(feat, cot, coords)


def neighbours(slab_coord, pos):
    row, col = pos // 4, lax.rem(pos, 4)
    slots = {}
    for dy in (-1, 0, 1):
        for dx in (-1, 0, 1):
            y, x = row + dy, col + dx
            inside = (y >= 0) & (y < 4) & (x >= 0) & (x < 4) & (pos < 16)
            wanted = jnp.where(inside, y * 4 + x, 99)
            slot = jnp.int32(SLOTS)
            for k in range(SLOTS):
                slot = jnp.where(slab_coord(k) == wanted, k, slot)
            slots[dy, dx] = slot
    return slots


def build_plane(get, slots, even, odd, i, z):
    lane_x = lax.broadcasted_iota(jnp.int32, (10, 8, C), 1)

    def column(dx):
        middle = get(slots[0, dx], 0, 64).astype(F32).reshape(8, 8, C)
        top = get(slots[-1, dx], 48, 16).astype(F32).reshape(2, 8, C)[1:]
        bottom = get(slots[1, dx], 0, 16).astype(F32).reshape(2, 8, C)[:1]
        return jnp.concatenate([top, middle, bottom], axis=0)

    left, centre, right = column(-1), column(0), column(1)
    before = pltpu.roll(jnp.where(lane_x == 7, left, centre), 1, 1)
    after = pltpu.roll(jnp.where(lane_x == 0, right, centre), 7, 1)
    for d, rows in enumerate((before, centre, after)):
        even[d, i, z] = rows[1:9].reshape(64, C).astype(BF)
        odd[d, i, z] = rows.reshape(80, C).astype(BF)


def shifted(even, odd, tap, flips, brick=None):
    tz, ty, tx = tap // 9, tap // 3 % 3, tap % 3
    flip_x, flip_y, flip_z = flips
    z0 = jnp.where(flip_z, 2 - tz, tz)
    x0 = jnp.where(flip_x, 2 - tx, tx)
    which = slice(None) if brick is None else brick
    count = SLOTS if brick is None else 1
    if ty == 1:
        cells = even[x0, which, pl.ds(z0, 8)]
    else:
        y0 = pl.multiple_of(jnp.where(flip_y, 2 - ty, ty) * 8, 16)
        cells = odd[x0, which, pl.ds(z0, 8), pl.ds(y0, 64)]
    return cells.reshape(count * CELLS, C)


def conv_kernel(
    coords, near_coords, code, feat, cot, kernel, hv, hu, out, dx, grad, V, U, HV, HU, KV, even_v, odd_v, even_u, odd_u, cot_t, sems
):
    loads = [
        pltpu.make_async_copy(feat, V.at[pl.ds(0, SLOTS)], sems.at[0]),
        pltpu.make_async_copy(hv, HV.at[:, pl.ds(0, SLOTS)], sems.at[1]),
        pltpu.make_async_copy(cot, U.at[pl.ds(0, SLOTS)], sems.at[2]),
        pltpu.make_async_copy(hu, HU.at[:, pl.ds(0, SLOTS)], sems.at[3]),
        pltpu.make_async_copy(kernel, KV, sems.at[4]),
    ]
    for load in loads:
        load.start()
    s = lax.axis_index("slab")
    for cells in (V, U):
        cells[SLOTS] = jnp.zeros((8, 64, C), BF)
    for planes in (HV, HU):
        for d in range(2):
            planes[d, SLOTS] = jnp.zeros((64, C), BF)
    flip_code = code[0]
    flips = (lax.rem(flip_code, 2) == 1, lax.rem(flip_code // 2, 2) == 1, lax.rem(flip_code // 4, 2) == 1)
    opposite = tuple(jnp.logical_not(f) for f in flips)

    def coord_of(d):
        if d == 1:
            return lambda k: coords[0, k]
        edge = (s == 0) if d == 0 else (s == 63)
        return lambda k: jnp.where(edge, 16, near_coords[d // 2, 0, k])

    def build(cells, planes, even, odd):
        @pl.loop(0, SLOTS)
        def _(i):
            slots = [neighbours(coord_of(d), coords[0, i]) for d in range(3)]

            @pl.loop(0, 8)
            def _(z):
                build_plane(lambda j, a, n: cells[j, z, pl.ds(a, n), :], slots[1], even, odd, i, z + 1)

            for d, z in ((0, 0), (1, 9)):
                build_plane(lambda j, a, n: planes[d, j, pl.ds(a, n), :], slots[2 * d], even, odd, i, z)

    loads[0].wait()
    loads[1].wait()
    build(V, HV, even_v, odd_v)
    loads[2].wait()
    for i in range(SLOTS):
        cells = jnp.where(coords[0, i] < 16, U[i].reshape(CELLS, C), jnp.zeros((), BF))
        cot_t[:, i * CELLS : (i + 1) * CELLS] = cells.T
    for first in range(0, TAPS, 2):
        taps = range(first, min(first + 2, TAPS))
        cols = jnp.concatenate([shifted(even_v, odd_v, t, flips) for t in taps], axis=1)
        sums = jnp.dot(cot_t[...], cols, preferred_element_type=F32)
        for n, t in enumerate(taps):
            grad[t * C : (t + 1) * C] = sums[:, n * C : (n + 1) * C].T
    grad[TAPS * C :] = jnp.zeros((4 * QROWS - TAPS * C, C), F32)
    loads[3].wait()
    build(U, HU, even_u, odd_u)
    loads[4].wait()

    @pl.loop(0, SLOTS)
    def _(i):
        active = coords[0, i] < 16
        for backward in (False, True):
            total = jnp.zeros((CELLS, C), F32)
            for first in range(0, TAPS, 2):
                taps = range(first, min(first + 2, TAPS))
                if backward:
                    cols = jnp.concatenate([shifted(even_u, odd_u, t, opposite, i) for t in taps], axis=1)
                    weights = jnp.concatenate([KV[t * C : (t + 1) * C] for t in taps], axis=1)
                    dims = (((1,), (1,)), ((), ()))
                else:
                    cols = jnp.concatenate([shifted(even_v, odd_v, t, flips, i) for t in taps], axis=1)
                    weights = KV[first * C : (first + len(taps)) * C]
                    dims = (((1,), (0,)), ((), ()))
                total += lax.dot_general(cols, weights, dims, preferred_element_type=F32)
            (dx if backward else out)[i] = jnp.where(active, total, 0.0).astype(BF).reshape(8, 64, C)


def convolve(coords, near_coords, code, feat, cot, kernel, hv, hu):
    smem, vmem = pl.BlockSpec(memory_space=pltpu.SMEM), pl.BlockSpec(memory_space=pltpu.VMEM)
    anywhere = pl.BlockSpec(memory_space=pl.ANY)
    cells, planes = pltpu.VMEM((SLOTS + 1, 8, 64, C), BF), pltpu.VMEM((2, SLOTS + 1, 64, C), BF)
    even, odd = pltpu.VMEM((3, SLOTS, 10, 64, C), BF), pltpu.VMEM((3, SLOTS, 10, 80, C), BF)
    return pl.pallas_call(
        conv_kernel,
        out_shape=[
            jax.ShapeDtypeStruct((SLOTS, 8, 64, C), BF),
            jax.ShapeDtypeStruct((SLOTS, 8, 64, C), BF),
            jax.ShapeDtypeStruct((4 * QROWS, C), F32),
        ],
        in_specs=[smem] * 3 + [anywhere] * 5,
        out_specs=[vmem] * 3,
        scratch_shapes=[cells, cells, planes, planes, pltpu.VMEM((TAPS * C, C), BF), even, odd, even, odd]
        + [pltpu.VMEM((C, SLOTS * CELLS), BF), pltpu.SemaphoreType.DMA((5,))],
        compiler_params=pltpu.CompilerParams(vmem_limit_bytes=48 << 20),
        name="brick_convs",
    )(coords, near_coords, code, feat, cot, kernel, hv, hu)


def encode(rows):
    index = lax.broadcasted_iota(jnp.int32, (32, C), 0)
    top = jnp.max(jnp.where(index < CHUNK, jnp.abs(rows), 0.0), axis=0, keepdims=True)
    power = jnp.ceil(jnp.log2(jnp.maximum(top, 2.0**-100)))
    codes = jnp.round(rows * jnp.exp2(BITS - power))
    codes = jnp.where(index < CHUNK, codes, jnp.broadcast_to(power, (32, C)))
    return codes.astype(jnp.int32).astype(jnp.int16)


def decode(codes):
    values = codes.astype(jnp.int32).astype(F32)
    return values * jnp.exp2(values[CHUNK : CHUNK + 1] - BITS)


def sum_kernel(grad, gathered, own, sibling, out_codes, in_codes, mid_codes, mid_in, sems, core_send, core_recv, s1, r1, s2, r2, s3, r3):
    z, x, core, y = place()
    me = (x * 8 + y, x * 8 + z)
    ring_me = (z, y)

    def group_device(part, j):
        if part == 0:
            return device(z, j // 8, core, lax.rem(j, 8))
        return device(lax.rem(j, 8), j // 8, core, y)

    def ring_device(part, j):
        return device(j, x, core, y) if part == 0 else device(z, x, core, j)

    other = device(z, x, 1 - core, y)
    barrier = pltpu.get_barrier_semaphore()
    pl.semaphore_signal(barrier, inc=1, device_id=other, device_id_type=MESH)
    for part in range(2):

        @pl.loop(1, GROUP)
        def _(k):
            peer = group_device(part, lax.rem(me[part] + k, GROUP))
            pl.semaphore_signal(barrier, inc=1, device_id=peer, device_id_type=MESH)

    pl.semaphore_wait(barrier, 1 + 2 * (GROUP - 1))

    core_copies, loads = [], []
    for part in range(2):
        theirs, mine = (2 * part + 1 - core) * QROWS, (2 * part + core) * QROWS
        core_copies.append(
            remote(
                grad.at[pl.ds(pl.multiple_of(theirs, 8), QROWS)],
                sibling.at[part, pl.ds(0, QROWS)],
                core_send.at[part],
                core_recv.at[part],
                other,
            )
        )
        loads.append(
            pltpu.make_async_copy(
                grad.at[pl.ds(pl.multiple_of(mine, 8), QROWS)], own.at[part, pl.ds(0, QROWS)], sems.at[part]
            )
        )
    for copy in core_copies + loads:
        copy.start()

    def scatter(part, k):
        j = lax.rem(me[part] + k, GROUP)
        return remote(
            out_codes.at[part, j],
            in_codes.at[part, me[part]],
            s1.at[part, j],
            r1.at[part, me[part]],
            group_device(part, j),
        )

    for part in range(2):
        loads[part].wait()
        core_copies[part].wait_recv()

        @pl.loop(0, GROUP // 2)
        def _(pair):
            base = pl.multiple_of(pair * 2 * CHUNK, 8)
            both = own[part, pl.ds(base, 64)] + sibling[part, pl.ds(base, 64)]
            out_codes[part, 2 * pair] = encode(both[:32])
            out_codes[part, 2 * pair + 1] = encode(both[CHUNK : CHUNK + 32])

        @pl.loop(1, GROUP)
        def _(k):
            scatter(part, k).start()

    def exchange(part, k):
        j = lax.rem(ring_me[part] + k, 8)
        return remote(
            mid_codes.at[part],
            mid_in.at[part, ring_me[part]],
            s2.at[part, j],
            r2.at[part, ring_me[part]],
            ring_device(part, j),
        )

    for part in range(2):

        def add(k, total):
            j = lax.rem(me[part] + k, GROUP)
            remote(
                out_codes.at[part, j], in_codes.at[part, j], s1.at[part, j], r1.at[part, j], group_device(part, j)
            ).wait_recv()
            return total + decode(in_codes[part, j])

        total = lax.fori_loop(1, GROUP, add, decode(out_codes[part, me[part]]))
        codes = encode(total)
        mid_codes[part] = codes
        mid_in[part, ring_me[part]] = codes

        @pl.loop(1, 8)
        def _(k):
            exchange(part, k).start()

    def publish(part, k):
        j = lax.rem(me[part] + k, GROUP)
        block = gathered.at[2 * part + core, me[part]]
        return remote(block, block, s3.at[part, j], r3.at[part, me[part]], group_device(part, j))

    for part in range(2):

        @pl.loop(1, 8)
        def _(k):
            j = lax.rem(ring_me[part] + k, 8)
            remote(
                mid_codes.at[part], mid_in.at[part, j], s2.at[part, j], r2.at[part, j], ring_device(part, j)
            ).wait_recv()

        total = decode(mid_in[part, 0])
        for j in range(1, 8):
            total += decode(mid_in[part, j])
        gathered[2 * part + core, me[part]] = encode(total)

        @pl.loop(1, GROUP)
        def _(k):
            publish(part, k).start()

    handed = []
    for part in range(2):

        @pl.loop(1, GROUP)
        def _(k):
            j = lax.rem(me[part] + k, GROUP)
            block = gathered.at[2 * part + core, j]
            remote(block, block, s3.at[part, j], r3.at[part, j], group_device(part, j)).wait_recv()

        block = gathered.at[2 * part + core]
        handed.append(remote(block, block, core_send.at[2 + part], core_recv.at[2 + part], other))
        handed[part].start()

    for part in range(2):
        core_copies[part].wait_send()

        @pl.loop(1, GROUP)
        def _(k):
            scatter(part, k).wait_send()
            publish(part, k).wait_send()

        @pl.loop(1, 8)
        def _(k):
            exchange(part, k).wait_send()

    for part in range(2):
        handed[part].wait_send()
        block = gathered.at[2 * part + 1 - core]
        remote(block, block, core_send.at[2 + part], core_recv.at[2 + part], other).wait_recv()


def sum_codes(grad):
    anywhere, vmem = pl.BlockSpec(memory_space=pl.ANY), pl.BlockSpec(memory_space=pltpu.VMEM)
    dma = pltpu.SemaphoreType.DMA
    return pl.pallas_call(
        sum_kernel,
        out_shape=jax.ShapeDtypeStruct((4, GROUP, 32, C), jnp.int16),
        in_specs=[anywhere],
        out_specs=vmem,
        scratch_shapes=[
            pltpu.VMEM((2, QROWS + 8, C), F32),
            pltpu.VMEM((2, QROWS + 8, C), F32),
            pltpu.VMEM((2, GROUP, 32, C), jnp.int16),
            pltpu.VMEM((2, GROUP, 32, C), jnp.int16),
            pltpu.VMEM((2, 32, C), jnp.int16),
            pltpu.VMEM((2, 8, 32, C), jnp.int16),
            dma((2,)),
            dma((4,)),
            dma((4,)),
            dma((2, GROUP)),
            dma((2, GROUP)),
            dma((2, 8)),
            dma((2, 8)),
            dma((2, GROUP)),
            dma((2, GROUP)),
        ],
        compiler_params=pltpu.CompilerParams(collective_id=1, has_side_effects=True, vmem_limit_bytes=32 << 20),
        name="sum_gradient",
    )(grad)


def decode_kernel(scale, codes, out):
    for q in range(4):

        @pl.loop(0, GROUP // 2 if q < 3 else 13)
        def _(pair):
            low = decode(codes[q, 2 * pair])[:CHUNK]
            high = decode(codes[q, 2 * pair + 1])[:CHUNK]
            start = pl.multiple_of(q * QROWS + pair * 2 * CHUNK, 8)
            out[pl.ds(start, 2 * CHUNK)] = jnp.concatenate([low, high], axis=0) * scale

    tail = jnp.concatenate([decode(codes[3, 26])[:CHUNK], decode(codes[3, 27])[:CHUNK]], axis=0) * scale
    out[pl.ds(3 * QROWS + 26 * CHUNK, 40)] = tail[:40]


def decode_all(codes, scale):
    vmem = pl.BlockSpec(memory_space=pltpu.VMEM)
    return pl.pallas_call(
        functools.partial(decode_kernel, scale),
        out_shape=jax.ShapeDtypeStruct((TAPS * C, C), F32),
        in_specs=[vmem],
        out_specs=vmem,
        compiler_params=pltpu.CompilerParams(vmem_limit_bytes=32 << 20),
        name="decode_gradient",
    )(codes)


def shards(features, cotangent, coords, orientation, kernel):
    feat = features.reshape(SLOTS, 8, 64, C)
    cot = cotangent.reshape(SLOTS, 8, 64, C)
    row = jnp.broadcast_to(jnp.pad(coords, ((0, 0), (0, C - SLOTS))), (8, C))
    hv, hu, hc = halo(feat, cot, row)
    out, dx, grad = convolve(coords, hc, orientation, feat, cot, kernel.reshape(TAPS * C, C), hv, hu)
    scale = float(8 * 64 * 2 * 512) ** -0.5
    total = decode_all(sum_codes(grad), scale)
    shape = (1, SLOTS, CELLS, C)
    return out.reshape(shape), dx.reshape(shape), total


def solution(mesh):
    in_specs = (
        P("batch", "slab", None, None),
        P("batch", "slab", None, None),
        P("batch", "slab"),
        P("batch"),
        P(),
    )
    out_specs = (P("batch", "slab", None, None), P("batch", "slab", None, None), P())
    return jax.shard_map(shards, mesh=mesh, in_specs=in_specs, out_specs=out_specs, check_vma=False)
```

time: 394 us -> 82.9 us (0.21)
  waiting for transfers between devices: 278 us -> 0 us
  Pallas kernels: 0 us -> 73.5 us
  local copies, waits for them, and re-layouts: 51.6 us -> 7.66 us
  matrix products: 19.9 us -> 0 us
  other arithmetic: 17.5 us -> 0 us
  between operations: 15 us -> 1.32 us
  starting transfers between devices: 11.1 us -> 0 us
    psum x1 -> x0, waiting for transfers between devices: 278 us -> none  [shards(): kernel_grad = lax.psum(local_grad, ('slab', 'batch'))]
    pallas_call x0 -> x4, Pallas kernels: none -> 73.5 us  [the longest x1 42.4 us: sum_codes(): pl.pallas_call(sum_kernel, out_shape=jax.ShapeDtypeStruct((4, GROUP, 32,...]
    dot_general x9 -> x0, matrix products: 19.9 us -> none  [the longest x2 5.66 us: brick_pass(): lax.dot_general(x_cols, centre, (((0,), (0,)), ((), ())), preferred_eleme...]
    concatenate x2 -> x0, other arithmetic: 13 us -> none  [the longest x1 13 us: shards(): jnp.concatenate([lower_plane[:, None], dense_slab, upper_plane[:, None]],...]
    while x124 -> x0, local copies, waits for them, and re-layouts: 12.1 us -> none
    ppermute x2 -> x0, starting transfers between devices: 11 us -> none  [the longest x1 6.54 us: padded_2(): lax.ppermute(head, axis, [((i + 1) % count, i) for i in range(ends)])]
    reshape x1 -> x0, local copies, waits for them, and re-layouts: 9.14 us -> none  [shards(): dense_slab.astype(jnp.bfloat16).reshape(2, B, G * B, G * B, channels)]
    gather x1 -> x0, local copies, waits for them, and re-layouts: 6.37 us -> none  [extract(): lax.dynamic_slice(padded, (0, 0, pos_row * B, pos_col * B, 0), (2, B + 2,...]
  transfers between devices with their start and end apart: 3 -> 0, of which waited for: 1 -> 0; matrix products, arithmetic and copies ran while one was open for 5% -> 0% of each run, Pallas kernels for 0% -> 0%
where the time goes in v1:
time: 82.9 us; the launch traced here: 82.5 us
  Pallas kernels  73.5 us (89%)
  local copies, waits for them, and re-layouts  7.66 us (9%)
  between operations  1.32 us (2%)
    pallas_call x1, Pallas kernels, sum_codes(): pl.pallas_call(sum_kernel, out_shape=jax.ShapeDtypeStruct((4, GROUP, 32,...  42.4 us
    pallas_call x1, Pallas kernels, convolve(): pl.pallas_call(conv_kernel, out_shape=[jax.ShapeDtypeStruct((SLOTS, 8, 64...  14.8 us
    pallas_call x1, Pallas kernels, halo(): pl.pallas_call(halo_kernel, out_shape=[jax.ShapeDtypeStruct((2, SLOTS, 64...  14.2 us
    unnamed x14, local copies, waits for them, and re-layouts  6.4 us
    pallas_call x1, Pallas kernels, decode_all(): pl.pallas_call(functools.partial(decode_kernel, scale), out_shape=jax.Sha...  2.18 us

profile of v1, /device:TPU:1, one launch (start us, length us, event | category | flops | bytes accessed | tf_op | source)
XLA Modules:
  0.0 82.5 jit_solution(8492565292954156324)
XLA Ops:
  1.3 0.7 pad_bitcast_fusion
  1.9 0.6 broadcast_in_dim.8.coords
  2.5 14.2 %halo_planes.1 = (bf16[2,4,64,128]{3,2,1,0:T(8,128)(2,1)}, bf16[2,4,64,128]{3,2,1,0:T(8,128)(2,1)}, s32[2,8,128]{2,1,0:T(8,128)}) custom-call(bf16[4,8,64,128]{3,2,1,0:T(8,128)(2,1)} %bitcast.7, bf16[4,8,64,128]{3,2,1,0:T(8,128)(2,1)} %bitcast.9, s32[8,128]{1,0:T(8,128)} %broadcast_in_dim.8.coords), custom_call_target="tpu_custom_call" | custom-call | tf_op jit(solution)/shard_map/halo_planes/pallas_call | solution.py:58
  16.7 0.0 copy-start
  16.7 1.0 %copy-done = bf16[1,4,512,128]{3,2,1,0:T(8,128)(2,1)S(1)} copy-done((bf16[1,4,512,128]{3,2,1,0:T(8,128)(2,1)S(1)}, bf16[1,4,512,128]{3,2,1,0:T(8,128)(2,1)}, u32[]{:S(2)}) %copy-start) | copy-done | bytes 524312
  17.8 0.0 copy-start.1
  17.8 1.0 %copy-done.1 = bf16[1,4,512,128]{3,2,1,0:T(8,128)(2,1)S(1)} copy-done((bf16[1,4,512,128]{3,2,1,0:T(8,128)(2,1)S(1)}, bf16[1,4,512,128]{3,2,1,0:T(8,128)(2,1)}, u32[]{:S(2)}) %copy-start.1) | copy-done | bytes 524312
  18.8 0.0 copy-start.2
  18.8 1.2 %copy-done.2 = bf16[27,128,128]{2,1,0:T(8,128)(2,1)S(1)} copy-done((bf16[27,128,128]{2,1,0:T(8,128)(2,1)S(1)}, bf16[27,128,128]{2,1,0:T(8,128)(2,1)}, u32[]{:S(2)}) %copy-start.2) | copy-done | bytes 884760
  20.0 0.0 copy-start.3
  20.0 0.9 %copy-done.3 = bf16[2,4,64,128]{3,2,1,0:T(8,128)(2,1)S(1)} copy-done((bf16[2,4,64,128]{3,2,1,0:T(8,128)(2,1)S(1)}, bf16[2,4,64,128]{3,2,1,0:T(8,128)(2,1)}, u32[]{:S(2)}) %copy-start.3) | copy-done | bytes 131096
  20.9 0.0 copy-start.4
  20.9 0.9 %copy-done.4 = bf16[2,4,64,128]{3,2,1,0:T(8,128)(2,1)S(1)} copy-done((bf16[2,4,64,128]{3,2,1,0:T(8,128)(2,1)S(1)}, bf16[2,4,64,128]{3,2,1,0:T(8,128)(2,1)}, u32[]{:S(2)}) %copy-start.4) | copy-done | bytes 131096
  21.8 0.0 copy-start.5
  21.8 0.7 copy-done.5
  22.5 0.0 copy-start.6
  22.5 0.7 copy-done.6
  23.1 14.8 %brick_convs.1 = (bf16[4,8,64,128]{3,2,1,0:T(8,128)(2,1)}, bf16[4,8,64,128]{3,2,1,0:T(8,128)(2,1)}, f32[3584,128]{1,0:T(8,128)S(1)}) custom-call(s32[1,4]{1,0:T(1,128)S(1)} %copy-done.6, s32[2,8,128]{2,1,0:T(8,128)S(1)} %copy-done.5, s32[1]{0:T(128)S(6)} %copy.8.code, bf16[4,8,64,128]{3,2,1,0:T(8,128)(2,1)S(1)} %bitcast.8, ...), custom_call_target="tpu_custom_call" | custom-call | tf_op jit(solution)/shard_map/brick_convs/pallas_call | solution.py:202
  37.9 42.4 %sum_gradient.1.codes = s16[4,32,32,128]{3,2,1,0:T(8,128)(2,1)S(1)} custom-call(f32[3584,128]{1,0:T(8,128)S(1)} %get-tuple-element.14.grad), custom_call_target="tpu_custom_call" | custom-call | tf_op jit(solution)/shard_map/sum_gradient/pallas_call | solution.py:387
  80.3 2.2 %decode_gradient.1 = f32[3456,128]{1,0:T(8,128)} custom-call(s16[4,32,32,128]{3,2,1,0:T(8,128)(2,1)S(1)} %sum_gradient.1.codes), custom_call_target="tpu_custom_call" | custom-call | tf_op jit(solution)/shard_map/decode_gradient/pallas_call | solution.py:430
Async XLA Ops:
  16.7 1.0 %copy-start = (bf16[1,4,512,128]{3,2,1,0:T(8,128)(2,1)S(1)}, bf16[1,4,512,128]{3,2,1,0:T(8,128)(2,1)}, u32[]{:S(2)}) copy-start(bf16[1,4,512,128]{3,2,1,0:T(8,128)(2,1)} %param.5) | copy-start | bytes 1572868
  17.8 1.0 %copy-start.1 = (bf16[1,4,512,128]{3,2,1,0:T(8,128)(2,1)S(1)}, bf16[1,4,512,128]{3,2,1,0:T(8,128)(2,1)}, u32[]{:S(2)}) copy-start(bf16[1,4,512,128]{3,2,1,0:T(8,128)(2,1)} %param.6) | copy-start | bytes 1572868
  18.8 1.2 %copy-start.2 = (bf16[27,128,128]{2,1,0:T(8,128)(2,1)S(1)}, bf16[27,128,128]{2,1,0:T(8,128)(2,1)}, u32[]{:S(2)}) copy-start(bf16[27,128,128]{2,1,0:T(8,128)(2,1)} %param.9) | copy-start | bytes 2654212
  20.0 0.9 %copy-start.3 = (bf16[2,4,64,128]{3,2,1,0:T(8,128)(2,1)S(1)}, bf16[2,4,64,128]{3,2,1,0:T(8,128)(2,1)}, u32[]{:S(2)}) copy-start(bf16[2,4,64,128]{3,2,1,0:T(8,128)(2,1)} %get-tuple-element.10.hv) | copy-start | bytes 393220
  20.9 0.9 %copy-start.4 = (bf16[2,4,64,128]{3,2,1,0:T(8,128)(2,1)S(1)}, bf16[2,4,64,128]{3,2,1,0:T(8,128)(2,1)}, u32[]{:S(2)}) copy-start(bf16[2,4,64,128]{3,2,1,0:T(8,128)(2,1)} %get-tuple-element.11.hu) | copy-start | bytes 393220
  21.8 0.7 copy-start.5
  22.5 0.7 copy-start.6

commit v2 on v0

v2 whole, which is shorter than its diff:
```python
import functools

import jax
import jax.numpy as jnp
from jax import lax
from jax.experimental import pallas as pl
from jax.experimental.pallas import tpu as pltpu
from jax.sharding import PartitionSpec as P

C = 128
SLOTS = 4
CELLS = 512
TAPS = 27
GROUP = 32
PARTS = 4
PART_TAPS = 7
CHUNK = PART_TAPS * C // 2 // GROUP
ROWS = 16
BITS = 14.95
MIDDLE, LOW, HIGH = list(range(9, 18)), list(range(9)), list(range(18, 27))
ORDER = [list(range(9, 16)), [16, 17, 0, 1, 2, 3, 4], [5, 6, 7, 8, 18, 19, 20], list(range(21, 27))]
BF = jnp.bfloat16
F32 = jnp.float32
MESH = pl.DeviceIdType.MESH


def place():
    s = lax.axis_index("slab")
    return s // 8, lax.rem(s // 2, 4), lax.rem(s, 2), lax.axis_index("batch")


def device(z, x, core, y):
    return {"slab": z * 8 + x * 2 + core, "batch": y}


def remote(src, dst, send, recv, where):
    return pltpu.make_async_remote_copy(
        src_ref=src, dst_ref=dst, send_sem=send, recv_sem=recv, device_id=where, device_id_type=MESH
    )


def neighbours(slab_coord, pos):
    row, col = pos // 4, lax.rem(pos, 4)
    slots = {}
    for dy in (-1, 0, 1):
        for dx in (-1, 0, 1):
            y, x = row + dy, col + dx
            inside = (y >= 0) & (y < 4) & (x >= 0) & (x < 4) & (pos < 16)
            wanted = jnp.where(inside, y * 4 + x, 99)
            slot = jnp.int32(SLOTS)
            for k in range(SLOTS):
                slot = jnp.where(slab_coord(k) == wanted, k, slot)
            slots[dy, dx] = slot
    return slots


def build_plane(get, slots, even, odd, i, z):
    lane_x = lax.broadcasted_iota(jnp.int32, (10, 8, C), 1)

    def column(dx):
        middle = get(slots[0, dx], 0, 64).astype(F32).reshape(8, 8, C)
        top = get(slots[-1, dx], 48, 16).astype(F32).reshape(2, 8, C)[1:]
        bottom = get(slots[1, dx], 0, 16).astype(F32).reshape(2, 8, C)[:1]
        return jnp.concatenate([top, middle, bottom], axis=0)

    left, centre, right = column(-1), column(0), column(1)
    before = pltpu.roll(jnp.where(lane_x == 7, left, centre), 1, 1)
    after = pltpu.roll(jnp.where(lane_x == 0, right, centre), 7, 1)
    for d, rows in enumerate((before, centre, after)):
        even[d, i, z] = rows[1:9].reshape(64, C).astype(BF)
        odd[d, i, z] = rows.reshape(80, C).astype(BF)


def shifted(even, odd, tap, brick=None):
    tz, ty, tx = tap // 9, tap // 3 % 3, tap % 3
    which = slice(None) if brick is None else brick
    count = SLOTS if brick is None else 1
    if ty == 1:
        cells = even[tx, which, tz : tz + 8]
    else:
        cells = odd[tx, which, tz : tz + 8, 8 * ty : 8 * ty + 64]
    return cells.reshape(count * CELLS, C)


def encode(rows):
    index = lax.broadcasted_iota(jnp.int32, (ROWS, C), 0)
    top = jnp.max(jnp.where(index < CHUNK, jnp.abs(rows), 0.0), axis=0, keepdims=True)
    power = jnp.ceil(jnp.log2(jnp.maximum(top, 2.0**-100)))
    codes = jnp.round(rows * jnp.exp2(BITS - power))
    codes = jnp.where(index < CHUNK, codes, jnp.broadcast_to(power, (ROWS, C)))
    return codes.astype(jnp.int32).astype(jnp.int16)


def decode(codes):
    values = codes.astype(jnp.int32).astype(F32)
    return values * jnp.exp2(values[CHUNK : CHUNK + 1] - BITS)


def main_kernel(
    coords, code, feat, cot, kernel, out, dx, gathered,
    V, U, HV, HU, HC, mine_c, near, KV, even_v, odd_v, even_u, odd_u, cot_t, edge_t, terms, grad, sibling,
    out_codes, in_codes, mid_codes, mid_in, OUT, DX,
    load_sem, halo_send, halo_recv, core_send, core_recv, s1, r1, s2, r2, s3, r3, hand_send, hand_recv, store_sem,
):
    slab = lax.axis_index("slab")
    z, x, core, y = place()
    me = (x * 8 + y, x * 8 + z)
    ring_me = (z, y)
    other = device(z, x, 1 - core, y)
    has_lower, has_upper = slab > 0, slab < 63
    lower, upper = {"slab": lax.rem(slab + 63, 64)}, {"slab": lax.rem(slab + 1, 64)}

    def group_device(kind, j):
        if kind == 0:
            return device(z, j // 8, core, lax.rem(j, 8))
        return device(lax.rem(j, 8), j // 8, core, y)

    def ring_device(kind, j):
        return device(j, x, core, y) if kind == 0 else device(z, x, core, j)

    barrier = pltpu.get_barrier_semaphore()
    pl.semaphore_signal(barrier, inc=1, device_id=other, device_id_type=MESH)

    @pl.when(has_upper & (core == 1))
    def _():
        pl.semaphore_signal(barrier, inc=1, device_id=upper, device_id_type=MESH)

    @pl.when(has_lower & (core == 0))
    def _():
        pl.semaphore_signal(barrier, inc=1, device_id=lower, device_id_type=MESH)

    for kind in range(2):

        @pl.loop(1, GROUP)
        def _(k):
            peer = group_device(kind, lax.rem(me[kind] + k, GROUP))
            pl.semaphore_signal(barrier, inc=1, device_id=peer, device_id_type=MESH)

    loads = [
        pltpu.make_async_copy(feat, V.at[pl.ds(0, SLOTS)], load_sem.at[0]),
        pltpu.make_async_copy(cot, U.at[pl.ds(0, SLOTS)], load_sem.at[1]),
        pltpu.make_async_copy(kernel, KV, load_sem.at[2]),
    ]
    for load in loads:
        load.start()
    for cells in (V, U):
        cells[SLOTS] = jnp.zeros((8, 64, C), BF)
    for planes in (HV, HU):
        for d in range(2):
            planes[d, SLOTS] = jnp.zeros((64, C), BF)
    for z0 in (0, 9):
        even_v[:, :, z0] = jnp.zeros((3, SLOTS, 64, C), BF)
        odd_v[:, :, z0] = jnp.zeros((3, SLOTS, 80, C), BF)
    lane = lax.broadcasted_iota(jnp.int32, (8, C), 1)
    row = jnp.full((8, C), 16, jnp.int32)
    for k in range(SLOTS):
        row = jnp.where(lane == k, coords[0, k], row)
    mine_c[...] = row
    flip_code = code[0]
    flip_x, flip_y, flip_z = lax.rem(flip_code, 2), lax.rem(flip_code // 2, 2), lax.rem(flip_code // 4, 2)

    def mirrored(tap):
        tz, ty, tx = tap // 9, tap // 3 % 3, tap % 3
        return tap + flip_z * (18 - 18 * tz) + flip_y * (6 - 6 * ty) + flip_x * (2 - 2 * tx)

    def inner(cells, even, odd):
        @pl.loop(0, SLOTS)
        def _(i):
            slots = neighbours(lambda k: coords[0, k], coords[0, i])

            @pl.loop(0, 8)
            def _(plane):
                build_plane(lambda j, a, n: cells[j, plane, pl.ds(a, n), :], slots, even, odd, i, plane + 1)

    def outer(planes, even, odd):
        @pl.loop(0, SLOTS)
        def _(i):
            for d, plane, there in ((0, 0, has_lower), (1, 9, has_upper)):
                slots = neighbours(lambda k: jnp.where(there, near[d, 0, k], 16), coords[0, i])
                build_plane(lambda j, a, n: planes[d, j, pl.ds(a, n), :], slots, even, odd, i, plane)

    loads[0].wait()
    inner(V, even_v, odd_v)
    loads[1].wait()
    zero = jnp.zeros((), BF)
    for i in range(SLOTS):
        cells = jnp.where(coords[0, i] < 16, U[i].reshape(CELLS, C), zero)
        cot_t[:, i * CELLS : (i + 1) * CELLS] = cells.T
    for d, plane in ((0, 0), (1, 7)):
        edge = [jnp.where(coords[0, i] < 16, U[i, plane], zero) for i in range(SLOTS)]
        edge_t[d] = jnp.concatenate(edge, axis=0).T
    def products(taps, left, read):
        for first in range(0, len(taps), 2):
            two = taps[first : first + 2]
            cols = jnp.concatenate([read(t) for t in two], axis=1)
            sums = jnp.dot(left, cols, preferred_element_type=F32)
            for k, t in enumerate(two):
                yield t, sums[:, k * C : (k + 1) * C].T

    def fill(part):
        for n, t in enumerate(ORDER[part]):
            grad[part, n * C : (n + 1) * C] = terms[mirrored(t)]

    for t, term in products(MIDDLE + LOW + HIGH, cot_t[...], lambda t: shifted(even_v, odd_v, t)):
        terms[t] = term
    fill(0)
    for n in range(len(ORDER[PARTS - 1]), PART_TAPS):
        grad[PARTS - 1, n * C : (n + 1) * C] = jnp.zeros((C, C), F32)

    half = PART_TAPS * C // 2

    def to_core(part):
        src = grad.at[part, pl.ds(pl.multiple_of((1 - core) * half, 8), half)]
        return remote(src, sibling.at[part, pl.ds(0, half)], core_send.at[part], core_recv.at[part], other)

    pl.semaphore_wait(barrier, 2 * GROUP - 1 + ((has_upper & (core == 1)) | (has_lower & (core == 0))).astype(jnp.int32))

    halos = []
    for d, (there, peer, plane) in enumerate(((has_upper, upper, 7), (has_lower, lower, 0))):
        group = [
            remote(mine_c, HC.at[d], halo_send.at[d, 0], halo_recv.at[d, 0], peer),
            remote(feat.at[:, plane], HV.at[d, pl.ds(0, SLOTS)], halo_send.at[d, 1], halo_recv.at[d, 1], peer),
            remote(cot.at[:, plane], HU.at[d, pl.ds(0, SLOTS)], halo_send.at[d, 2], halo_recv.at[d, 2], peer),
        ]
        halos.append((there, group))

    def start_halo(k):
        for there, group in halos:
            pl.when(there)(group[k].start)

    def end_halo(k):
        for (there, _), (_, group) in zip(reversed(halos), halos, strict=True):
            pl.when(there)(group[k].wait_recv)

    start_halo(0)
    start_halo(1)
    to_core(0).start()
    start_halo(2)

    def scatter(part, k):
        kind = part % 2
        j = lax.rem(me[kind] + k, GROUP)
        return remote(
            out_codes.at[part, j], in_codes.at[part, me[kind]], s1.at[part], r1.at[part], group_device(kind, j)
        )

    def send_part(part):
        to_core(part).wait_recv()

        @pl.loop(0, GROUP // 4)
        def _(four):
            base = pl.multiple_of(four * 4 * CHUNK, 8)
            mine = grad[part, pl.ds(pl.multiple_of(core * half + base, 8), 64)]
            rows = mine + sibling[part, pl.ds(base, 64)]
            for n in range(4):
                out_codes[part, 4 * four + n] = encode(rows[n * CHUNK : n * CHUNK + ROWS])

        @pl.loop(1, GROUP)
        def _(k):
            scatter(part, k).start()

    send_part(0)

    end_halo(0)
    near_copy = pltpu.make_async_copy(HC, near, load_sem.at[3])
    near_copy.start()
    end_halo(1)
    near_copy.wait()
    outer(HV, even_v, odd_v)

    def edge_cells(t):
        ty, tx, side = t // 3 % 3, t % 3, 9 * (t // 18)
        if ty == 1:
            return even_v[tx, :, side].reshape(SLOTS * 64, C)
        return odd_v[tx, :, side, 8 * ty : 8 * ty + 64].reshape(SLOTS * 64, C)

    for d, taps in enumerate((LOW, HIGH)):
        for t, term in products(taps, edge_t[d], edge_cells):
            terms[t] += term
    for part in range(1, PARTS):
        fill(part)
        to_core(part).start()
    for part in range(1, PARTS):
        send_part(part)

    def convolve(i, backward):
        total = jnp.zeros((CELLS, C), F32)
        for first in range(0, TAPS, 2):
            taps = range(first, min(first + 2, TAPS))
            if backward:
                cols = jnp.concatenate([shifted(even_u, odd_u, 26 - t, i) for t in taps], axis=1)
                weights = jnp.concatenate([KV[mirrored(t)] for t in taps], axis=1)
                dims = (((1,), (1,)), ((), ()))
            else:
                cols = jnp.concatenate([shifted(even_v, odd_v, t, i) for t in taps], axis=1)
                weights = jnp.concatenate([KV[mirrored(t)] for t in taps], axis=0)
                dims = (((1,), (0,)), ((), ()))
            total += lax.dot_general(cols, weights, dims, preferred_element_type=F32)
        return jnp.where(coords[0, i] < 16, total, 0.0).astype(BF).reshape(8, 64, C)

    loads[2].wait()

    @pl.loop(0, SLOTS)
    def _(i):
        OUT[i] = convolve(i, False)

    out_copy = pltpu.make_async_copy(OUT, out, store_sem.at[0])
    out_copy.start()
    inner(U, even_u, odd_u)
    end_halo(2)
    outer(HU, even_u, odd_u)

    def exchange(part, k):
        kind = part % 2
        j = lax.rem(ring_me[kind] + k, 8)
        return remote(
            mid_codes.at[part], mid_in.at[part, ring_me[kind]], s2.at[part], r2.at[part], ring_device(kind, j)
        )

    def several(buffer, count, send, recv):
        blocks = buffer.at[pl.ds(0, count)]
        return remote(blocks, blocks, send, recv, other)

    for part in range(PARTS):
        kind = part % 2
        several(in_codes.at[part], GROUP - 1, s1.at[part], r1.at[part]).wait_recv()

        def add(k, total):
            return total + decode(in_codes[part, lax.rem(me[kind] + k, GROUP)])

        total = lax.fori_loop(1, GROUP, add, decode(out_codes[part, me[kind]]))
        codes = encode(total)
        mid_codes[part] = codes
        mid_in[part, ring_me[kind]] = codes

        @pl.loop(1, 8)
        def _(k):
            exchange(part, k).start()

    @pl.loop(0, 2)
    def _(i):
        DX[i] = convolve(i, True)

    def publish(part, k):
        kind = part % 2
        block = gathered.at[part, core, me[kind]]
        return remote(block, block, s3.at[part], r3.at[part], group_device(kind, lax.rem(me[kind] + k, GROUP)))

    for part in range(PARTS):
        kind = part % 2
        several(mid_in.at[part], 7, s2.at[part], r2.at[part]).wait_recv()
        total = decode(mid_in[part, 0])
        for j in range(1, 8):
            total += decode(mid_in[part, j])
        gathered[part, core, me[kind]] = encode(total)

        @pl.loop(1, GROUP)
        def _(k):
            publish(part, k).start()

    @pl.loop(2, SLOTS)
    def _(i):
        DX[i] = convolve(i, True)

    dx_copy = pltpu.make_async_copy(DX, dx, store_sem.at[1])
    dx_copy.start()

    def hand(part):
        block = gathered.at[part, core]
        return remote(block, block, hand_send.at[part], hand_recv.at[part], other)

    for part in range(PARTS):
        several(gathered.at[part, core], GROUP - 1, s3.at[part], r3.at[part]).wait_recv()
        hand(part).start()

    for part in range(PARTS):
        to_core(part).wait_send()
        several(out_codes.at[part], GROUP - 1, s1.at[part], r1.at[part]).wait_send()
        several(mid_in.at[part], 7, s2.at[part], r2.at[part]).wait_send()
        several(gathered.at[part, core], GROUP - 1, s3.at[part], r3.at[part]).wait_send()
        hand(part).wait_send()
    for there, group in halos:
        for copy in group:
            pl.when(there)(copy.wait_send)
    out_copy.wait()
    dx_copy.wait()
    for part in range(PARTS):
        hand(part).wait_recv()


def main_call(coords, code, feat, cot, kernel):
    smem, vmem = pl.BlockSpec(memory_space=pltpu.SMEM), pl.BlockSpec(memory_space=pltpu.VMEM)
    anywhere = pl.BlockSpec(memory_space=pl.ANY)
    dma = pltpu.SemaphoreType.DMA
    cells, planes = pltpu.VMEM((SLOTS + 1, 8, 64, C), BF), pltpu.VMEM((2, SLOTS + 1, 64, C), BF)
    even, odd = pltpu.VMEM((3, SLOTS, 10, 64, C), BF), pltpu.VMEM((3, SLOTS, 10, 80, C), BF)
    bricks = pltpu.VMEM((SLOTS, 8, 64, C), BF)
    codes = pltpu.VMEM((PARTS, GROUP, ROWS, C), jnp.int16)
    return pl.pallas_call(
        main_kernel,
        out_shape=[
            jax.ShapeDtypeStruct((SLOTS, 8, 64, C), BF),
            jax.ShapeDtypeStruct((SLOTS, 8, 64, C), BF),
            jax.ShapeDtypeStruct((PARTS, 2, GROUP, ROWS, C), jnp.int16),
        ],
        in_specs=[smem] * 2 + [anywhere] * 3,
        out_specs=[anywhere, anywhere, vmem],
        scratch_shapes=[
            cells, cells, planes, planes, pltpu.VMEM((2, 8, C), jnp.int32), pltpu.VMEM((8, C), jnp.int32),
            pltpu.SMEM((2, 8, C), jnp.int32), pltpu.VMEM((TAPS, C, C), BF), even, odd, even, odd,
            pltpu.VMEM((C, SLOTS * CELLS), BF), pltpu.VMEM((2, C, SLOTS * 64), BF), pltpu.VMEM((TAPS, C, C), F32),
            pltpu.VMEM((PARTS, PART_TAPS * C + 8, C), F32), pltpu.VMEM((PARTS, PART_TAPS * C // 2 + 8, C), F32),
            codes, codes, pltpu.VMEM((PARTS, ROWS, C), jnp.int16), pltpu.VMEM((PARTS, 8, ROWS, C), jnp.int16),
            bricks, bricks,
            dma((4,)), dma((2, 3)), dma((2, 3)), dma((PARTS,)), dma((PARTS,)), dma((PARTS,)), dma((PARTS,)),
            dma((PARTS,)), dma((PARTS,)), dma((PARTS,)), dma((PARTS,)), dma((PARTS,)), dma((PARTS,)), dma((2,)),
        ],
        compiler_params=pltpu.CompilerParams(collective_id=0, has_side_effects=True, vmem_limit_bytes=58 << 20),
        name="brick_convs",
    )(coords, code, feat, cot, kernel)


def result_kernel(scale, out_in, dx_in, codes, out, dx, grad, held, rows, bricks, sems):
    loads = [pltpu.make_async_copy(codes.at[p], held.at[p], sems.at[2 + p]) for p in range(PARTS)]
    passed = [(out_in, out), (dx_in, dx)]
    fetches = [pltpu.make_async_copy(src, bricks.at[k], sems.at[k]) for k, (src, _) in enumerate(passed)]
    copies = [pltpu.make_async_copy(bricks.at[k], dst, sems.at[k]) for k, (_, dst) in enumerate(passed)]
    for load in loads + fetches:
        load.start()
    half = PART_TAPS * C // 2
    stores = []
    for part in range(PARTS):
        if part >= 2:
            fetches[part - 2].wait()
            copies[part - 2].start()
        loads[part].wait()
        for core in range(2):

            @pl.loop(0, GROUP // 4)
            def _(four):
                blocks = [decode(held[part, core, 4 * four + n])[:CHUNK] for n in range(4)]
                start = pl.multiple_of(core * half + four * 4 * CHUNK, 8)
                rows[part, pl.ds(start, 4 * CHUNK)] = jnp.concatenate(blocks, axis=0) * scale

        first = 0
        taps = ORDER[part]
        for n in range(1, len(taps) + 1):
            if n == len(taps) or taps[n] != taps[n - 1] + 1:
                store = pltpu.make_async_copy(
                    rows.at[part, pl.ds(first * C, (n - first) * C)],
                    grad.at[pl.ds(taps[first] * C, (n - first) * C)],
                    sems.at[2 + PARTS + len(stores)],
                )
                store.start()
                stores.append(store)
                first = n
    for copy in stores + copies:
        copy.wait()


def results(out, dx, codes, scale):
    anywhere = pl.BlockSpec(memory_space=pl.ANY)
    return pl.pallas_call(
        functools.partial(result_kernel, scale),
        out_shape=[
            jax.ShapeDtypeStruct((SLOTS, 8, 64, C), BF),
            jax.ShapeDtypeStruct((SLOTS, 8, 64, C), BF),
            jax.ShapeDtypeStruct((TAPS * C, C), F32),
        ],
        in_specs=[anywhere] * 3,
        out_specs=[anywhere] * 3,
        scratch_shapes=[
            pltpu.VMEM((PARTS, 2, GROUP, ROWS, C), jnp.int16),
            pltpu.VMEM((PARTS, PART_TAPS * C, C), F32),
            pltpu.VMEM((2, SLOTS, 8, 64, C), BF),
            pltpu.SemaphoreType.DMA((2 + 4 * PARTS,)),
        ],
        compiler_params=pltpu.CompilerParams(vmem_limit_bytes=58 << 20),
        name="results",
    )(out, dx, codes)


def shards(features, cotangent, coords, orientation, kernel):
    feat = features.reshape(SLOTS, 8, 64, C)
    cot = cotangent.reshape(SLOTS, 8, 64, C)
    out, dx, codes = main_call(coords, orientation, feat, cot, kernel)
    out, dx, total = results(out, dx, codes, float(8 * 64 * 2 * 512) ** -0.5)
    shape = (1, SLOTS, CELLS, C)
    return out.reshape(shape), dx.reshape(shape), total


def solution(mesh):
    in_specs = (
        P("batch", "slab", None, None),
        P("batch", "slab", None, None),
        P("batch", "slab"),
        P("batch"),
        P(),
    )
    out_specs = (P("batch", "slab", None, None), P("batch", "slab", None, None), P())
    return jax.shard_map(shards, mesh=mesh, in_specs=in_specs, out_specs=out_specs, check_vma=False)
```

time: 394 us -> 55.7 us (0.14)
  waiting for transfers between devices: 278 us -> 0 us
  Pallas kernels: 0 us -> 54.3 us
  local copies, waits for them, and re-layouts: 51.6 us -> 0 us
  matrix products: 19.9 us -> 0 us
  other arithmetic: 17.5 us -> 0 us
  between operations: 15 us -> 1.29 us
  starting transfers between devices: 11.1 us -> 0 us
    psum x1 -> x0, waiting for transfers between devices: 278 us -> none  [shards(): kernel_grad = lax.psum(local_grad, ('slab', 'batch'))]
    pallas_call x0 -> x2, Pallas kernels: none -> 54.3 us  [the longest x1 51.2 us: main_call(): pl.pallas_call(main_kernel, out_shape=[jax.ShapeDtypeStruct((SLOTS, 8, 64...]
    dot_general x9 -> x0, matrix products: 19.9 us -> none  [the longest x2 5.66 us: brick_pass(): lax.dot_general(x_cols, centre, (((0,), (0,)), ((), ())), preferred_eleme...]
    concatenate x2 -> x0, other arithmetic: 13 us -> none  [the longest x1 13 us: shards(): jnp.concatenate([lower_plane[:, None], dense_slab, upper_plane[:, None]],...]
    while x124 -> x0, local copies, waits for them, and re-layouts: 12.1 us -> none
    ppermute x2 -> x0, starting transfers between devices: 11 us -> none  [the longest x1 6.54 us: padded_2(): lax.ppermute(head, axis, [((i + 1) % count, i) for i in range(ends)])]
    reshape x1 -> x0, local copies, waits for them, and re-layouts: 9.14 us -> none  [shards(): dense_slab.astype(jnp.bfloat16).reshape(2, B, G * B, G * B, channels)]
    gather x1 -> x0, local copies, waits for them, and re-layouts: 6.37 us -> none  [extract(): lax.dynamic_slice(padded, (0, 0, pos_row * B, pos_col * B, 0), (2, B + 2,...]
  transfers between devices with their start and end apart: 3 -> 0, of which waited for: 1 -> 0; matrix products, arithmetic and copies ran while one was open for 5% -> 0% of each run, Pallas kernels for 0% -> 0%
where the time goes in v2:
time: 55.7 us; the launch traced here: 55.6 us
  Pallas kernels  54.3 us (97%)
  between operations  1.29 us (2%)
    pallas_call x1, Pallas kernels, main_call(): pl.pallas_call(main_kernel, out_shape=[jax.ShapeDtypeStruct((SLOTS, 8, 64...  51.2 us
    pallas_call x1, Pallas kernels, results(): pl.pallas_call(functools.partial(result_kernel, scale), out_shape=[jax.Sh...  3.03 us

profile of v2, /device:TPU:1, one launch (start us, length us, event | category | flops | bytes accessed | tf_op | source)
XLA Modules:
  0.0 55.6 jit_solution(903092227295380292)
XLA Ops:
  1.3 51.2 %brick_convs.1 = (bf16[4,8,64,128]{3,2,1,0:T(8,128)(2,1)}, bf16[4,8,64,128]{3,2,1,0:T(8,128)(2,1)}, s16[4,2,32,16,128]{4,3,2,1,0:T(8,128)(2,1)}) custom-call(s32[1,4]{1,0:T(1,128)} %coords.1, s32[1]{0:T(128)S(6)} %copy.8.code, bf16[4,8,64,128]{3,2,1,0:T(8,128)(2,1)} %bitcast.4, bf16[4,8,64,128]{3,2,1,0:T(8,128)(2,1)} %bitcast.5, bf16[27,128,128]{2,1,0:T(8,128)(2,1)} %kernel.1), custom_call_target="tpu_custom_call" | custom-call | tf_op jit(solution)/shard_map/brick_convs/pallas_call | solution.py:399
  52.5 3.0 %results.1 = (bf16[4,8,64,128]{3,2,1,0:T(8,128)(2,1)}, bf16[4,8,64,128]{3,2,1,0:T(8,128)(2,1)}, f32[3456,128]{1,0:T(8,128)}) custom-call(bf16[4,8,64,128]{3,2,1,0:T(8,128)(2,1)} %get-tuple-element.9.out_in, bf16[4,8,64,128]{3,2,1,0:T(8,128)(2,1)} %get-tuple-element.10.dx_in, s16[4,2,32,16,128]{4,3,2,1,0:T(8,128)(2,1)} %get-tuple-element.11.codes), custom_call_target="tpu_custom_call" | custom-call | tf_op jit(solution)/shard_map/results/pallas_call | solution.py:463

commit v3 on v2

--- a/solution.py
+++ b/solution.py
@@ -26,7 +26,7 @@
 
 def place():
     s = lax.axis_index("slab")
-    return s // 8, lax.rem(s // 2, 4), lax.rem(s, 2), lax.axis_index("batch")
+    return s // 8, (s // 2) & 3, s & 1, lax.axis_index("batch")
 
 
 def device(z, x, core, y):
@@ -40,7 +40,7 @@
 
 
 def neighbours(slab_coord, pos):
-    row, col = pos // 4, lax.rem(pos, 4)
+    row, col = pos >> 2, pos & 3
     slots = {}
     for dy in (-1, 0, 1):
         for dx in (-1, 0, 1):
@@ -83,40 +83,48 @@
 
 
 def encode(rows):
-    index = lax.broadcasted_iota(jnp.int32, (ROWS, C), 0)
-    top = jnp.max(jnp.where(index < CHUNK, jnp.abs(rows), 0.0), axis=0, keepdims=True)
+    index = lax.broadcasted_iota(jnp.int32, rows.shape, 1)
+    top = jnp.max(jnp.where(index < CHUNK, jnp.abs(rows), 0.0), axis=1, keepdims=True)
     power = jnp.ceil(jnp.log2(jnp.maximum(top, 2.0**-100)))
     codes = jnp.round(rows * jnp.exp2(BITS - power))
-    codes = jnp.where(index < CHUNK, codes, jnp.broadcast_to(power, (ROWS, C)))
+    codes = jnp.where(index < CHUNK, codes, jnp.broadcast_to(power, rows.shape))
     return codes.astype(jnp.int32).astype(jnp.int16)
 
 
 def decode(codes):
     values = codes.astype(jnp.int32).astype(F32)
-    return values * jnp.exp2(values[CHUNK : CHUNK + 1] - BITS)
+    return values * jnp.exp2(values[:, CHUNK : CHUNK + 1] - BITS)
 
 
 def main_kernel(
     coords, code, feat, cot, kernel, out, dx, gathered,
     V, U, HV, HU, HC, mine_c, near, KV, even_v, odd_v, even_u, odd_u, cot_t, edge_t, terms, grad, sibling,
-    out_codes, in_codes, mid_codes, mid_in, OUT, DX,
-    load_sem, halo_send, halo_recv, core_send, core_recv, s1, r1, s2, r2, s3, r3, hand_send, hand_recv, store_sem,
+    out_codes, in_codes, mid_codes, mid_in,
+    load_sem, halo_send, halo_recv, core_send, core_recv, s1, r1, s2, r2, s3, r3, hand_send, hand_recv,
 ):
     slab = lax.axis_index("slab")
     z, x, core, y = place()
     me = (x * 8 + y, x * 8 + z)
     ring_me = (z, y)
+
     other = device(z, x, 1 - core, y)
     has_lower, has_upper = slab > 0, slab < 63
     lower, upper = {"slab": lax.rem(slab + 63, 64)}, {"slab": lax.rem(slab + 1, 64)}
 
-    def group_device(kind, j):
-        if kind == 0:
-            return device(z, j // 8, core, lax.rem(j, 8))
-        return device(lax.rem(j, 8), j // 8, core, y)
-
-    def ring_device(kind, j):
-        return device(j, x, core, y) if kind == 0 else device(z, x, core, j)
+    near_x = [(x + step) & 3 for step in range(4)]
+    near_y, near_z = [(y + step) & 7 for step in range(8)], [(z + step) & 7 for step in range(8)]
+
+    def team(kind):
+        for step_x in range(4):
+            for step in range(8):
+                if step_x or step:
+                    row, column = near_x[step_x], (near_y, near_z)[kind][step]
+                    where = device(z, row, core, column) if kind == 0 else device(column, row, core, y)
+                    yield row * 8 + column, where
+
+    def ring(kind):
+        for step in range(1, 8):
+            yield device(near_z[step], x, core, y) if kind == 0 else device(z, x, core, near_y[step])
 
     barrier = pltpu.get_barrier_semaphore()
     pl.semaphore_signal(barrier, inc=1, device_id=other, device_id_type=MESH)
@@ -130,10 +138,7 @@
         pl.semaphore_signal(barrier, inc=1, device_id=lower, device_id_type=MESH)
 
     for kind in range(2):
-
-        @pl.loop(1, GROUP)
-        def _(k):
-            peer = group_device(kind, lax.rem(me[kind] + k, GROUP))
+        for _, peer in team(kind):
             pl.semaphore_signal(barrier, inc=1, device_id=peer, device_id_type=MESH)
 
     loads = [
@@ -157,7 +162,7 @@
         row = jnp.where(lane == k, coords[0, k], row)
     mine_c[...] = row
     flip_code = code[0]
-    flip_x, flip_y, flip_z = lax.rem(flip_code, 2), lax.rem(flip_code // 2, 2), lax.rem(flip_code // 4, 2)
+    flip_x, flip_y, flip_z = flip_code & 1, (flip_code >> 1) & 1, (flip_code >> 2) & 1
 
     def mirrored(tap):
         tz, ty, tx = tap // 9, tap // 3 % 3, tap % 3
@@ -213,6 +218,7 @@
         src = grad.at[part, pl.ds(pl.multiple_of((1 - core) * half, 8), half)]
         return remote(src, sibling.at[part, pl.ds(0, half)], core_send.at[part], core_recv.at[part], other)
 
+    inner(U, even_u, odd_u)
     pl.semaphore_wait(barrier, 2 * GROUP - 1 + ((has_upper & (core == 1)) | (has_lower & (core == 0))).astype(jnp.int32))
 
     halos = []
@@ -237,27 +243,23 @@
     to_core(0).start()
     start_halo(2)
 
-    def scatter(part, k):
-        kind = part % 2
-        j = lax.rem(me[kind] + k, GROUP)
-        return remote(
-            out_codes.at[part, j], in_codes.at[part, me[kind]], s1.at[part], r1.at[part], group_device(kind, j)
-        )
+    def scatter(part):
+        landing = in_codes.at[part, me[part % 2]]
+        for j, peer in team(part % 2):
+            remote(out_codes.at[part, j], landing, s1.at[part], r1.at[part], peer).start()
 
     def send_part(part):
         to_core(part).wait_recv()
 
-        @pl.loop(0, GROUP // 4)
-        def _(four):
-            base = pl.multiple_of(four * 4 * CHUNK, 8)
-            mine = grad[part, pl.ds(pl.multiple_of(core * half + base, 8), 64)]
-            rows = mine + sibling[part, pl.ds(base, 64)]
-            for n in range(4):
-                out_codes[part, 4 * four + n] = encode(rows[n * CHUNK : n * CHUNK + ROWS])
-
-        @pl.loop(1, GROUP)
-        def _(k):
-            scatter(part, k).start()
+        @pl.loop(0, GROUP // 8)
+        def _(eight):
+            base = pl.multiple_of(eight * 8 * CHUNK, 8)
+            mine = grad[part, pl.ds(pl.multiple_of(core * half + base, 8), 120)]
+            rows = mine + sibling[part, pl.ds(base, 120)]
+            blocks = jnp.stack([rows[n * CHUNK : n * CHUNK + ROWS] for n in range(8)])
+            out_codes[part, pl.ds(eight * 8, 8)] = encode(blocks)
+
+        scatter(part)
 
     send_part(0)
 
@@ -302,20 +304,15 @@
 
     @pl.loop(0, SLOTS)
     def _(i):
-        OUT[i] = convolve(i, False)
-
-    out_copy = pltpu.make_async_copy(OUT, out, store_sem.at[0])
-    out_copy.start()
-    inner(U, even_u, odd_u)
+        out[i] = convolve(i, False)
+
     end_halo(2)
     outer(HU, even_u, odd_u)
 
-    def exchange(part, k):
-        kind = part % 2
-        j = lax.rem(ring_me[kind] + k, 8)
-        return remote(
-            mid_codes.at[part], mid_in.at[part, ring_me[kind]], s2.at[part], r2.at[part], ring_device(kind, j)
-        )
+    def exchange(part):
+        landing = mid_in.at[part, ring_me[part % 2]]
+        for peer in ring(part % 2):
+            remote(mid_codes.at[part], landing, s2.at[part], r2.at[part], peer).start()
 
     def several(buffer, count, send, recv):
         blocks = buffer.at[pl.ds(0, count)]
@@ -325,45 +322,38 @@
         kind = part % 2
         several(in_codes.at[part], GROUP - 1, s1.at[part], r1.at[part]).wait_recv()
 
-        def add(k, total):
-            return total + decode(in_codes[part, lax.rem(me[kind] + k, GROUP)])
-
-        total = lax.fori_loop(1, GROUP, add, decode(out_codes[part, me[kind]]))
-        codes = encode(total)
+        in_codes[part, me[kind]] = out_codes[part, me[kind]]
+
+        def add(eight, total):
+            return total + jnp.sum(decode(in_codes[part, pl.ds(eight * 8, 8)]), axis=0, keepdims=True)
+
+        total = lax.fori_loop(0, GROUP // 8, add, jnp.zeros((1, ROWS, C), F32))
+        codes = encode(total)[0]
         mid_codes[part] = codes
         mid_in[part, ring_me[kind]] = codes
 
-        @pl.loop(1, 8)
-        def _(k):
-            exchange(part, k).start()
+        exchange(part)
 
     @pl.loop(0, 2)
     def _(i):
-        DX[i] = convolve(i, True)
-
-    def publish(part, k):
-        kind = part % 2
-        block = gathered.at[part, core, me[kind]]
-        return remote(block, block, s3.at[part], r3.at[part], group_device(kind, lax.rem(me[kind] + k, GROUP)))
+        dx[i] = convolve(i, True)
+
+    def publish(part):
+        block = gathered.at[part, core, me[part % 2]]
+        for _, peer in team(part % 2):
+            remote(block, block, s3.at[part], r3.at[part], peer).start()
 
     for part in range(PARTS):
         kind = part % 2
         several(mid_in.at[part], 7, s2.at[part], r2.at[part]).wait_recv()
-        total = decode(mid_in[part, 0])
-        for j in range(1, 8):
-            total += decode(mid_in[part, j])
-        gathered[part, core, me[kind]] = encode(total)
-
-        @pl.loop(1, GROUP)
-        def _(k):
-            publish(part, k).start()
+        total = jnp.sum(decode(mid_in[part]), axis=0, keepdims=True)
+        gathered[part, core, me[kind]] = encode(total)[0]
+
+        publish(part)
 
     @pl.loop(2, SLOTS)
     def _(i):
-        DX[i] = convolve(i, True)
-
-    dx_copy = pltpu.make_async_copy(DX, dx, store_sem.at[1])
-    dx_copy.start()
+        dx[i] = convolve(i, True)
 
     def hand(part):
         block = gathered.at[part, core]
@@ -382,8 +372,6 @@
     for there, group in halos:
         for copy in group:
             pl.when(there)(copy.wait_send)
-    out_copy.wait()
-    dx_copy.wait()
     for part in range(PARTS):
         hand(part).wait_recv()
 
@@ -394,53 +382,44 @@
     dma = pltpu.SemaphoreType.DMA
     cells, planes = pltpu.VMEM((SLOTS + 1, 8, 64, C), BF), pltpu.VMEM((2, SLOTS + 1, 64, C), BF)
     even, odd = pltpu.VMEM((3, SLOTS, 10, 64, C), BF), pltpu.VMEM((3, SLOTS, 10, 80, C), BF)
-    bricks = pltpu.VMEM((SLOTS, 8, 64, C), BF)
     codes = pltpu.VMEM((PARTS, GROUP, ROWS, C), jnp.int16)
     return pl.pallas_call(
         main_kernel,
         out_shape=[
-            jax.ShapeDtypeStruct((SLOTS, 8, 64, C), BF),
-            jax.ShapeDtypeStruct((SLOTS, 8, 64, C), BF),
-            jax.ShapeDtypeStruct((PARTS, 2, GROUP, ROWS, C), jnp.int16),
+            pltpu.VMEM((SLOTS, 8, 64, C), BF),
+            pltpu.VMEM((SLOTS, 8, 64, C), BF),
+            pltpu.VMEM((PARTS, 2, GROUP, ROWS, C), jnp.int16),
         ],
         in_specs=[smem] * 2 + [anywhere] * 3,
-        out_specs=[anywhere, anywhere, vmem],
+        out_specs=[vmem] * 3,
         scratch_shapes=[
             cells, cells, planes, planes, pltpu.VMEM((2, 8, C), jnp.int32), pltpu.VMEM((8, C), jnp.int32),
             pltpu.SMEM((2, 8, C), jnp.int32), pltpu.VMEM((TAPS, C, C), BF), even, odd, even, odd,
             pltpu.VMEM((C, SLOTS * CELLS), BF), pltpu.VMEM((2, C, SLOTS * 64), BF), pltpu.VMEM((TAPS, C, C), F32),
             pltpu.VMEM((PARTS, PART_TAPS * C + 8, C), F32), pltpu.VMEM((PARTS, PART_TAPS * C // 2 + 8, C), F32),
             codes, codes, pltpu.VMEM((PARTS, ROWS, C), jnp.int16), pltpu.VMEM((PARTS, 8, ROWS, C), jnp.int16),
-            bricks, bricks,
             dma((4,)), dma((2, 3)), dma((2, 3)), dma((PARTS,)), dma((PARTS,)), dma((PARTS,)), dma((PARTS,)),
-            dma((PARTS,)), dma((PARTS,)), dma((PARTS,)), dma((PARTS,)), dma((PARTS,)), dma((PARTS,)), dma((2,)),
+            dma((PARTS,)), dma((PARTS,)), dma((PARTS,)), dma((PARTS,)), dma((PARTS,)), dma((PARTS,)),
         ],
-        compiler_params=pltpu.CompilerParams(collective_id=0, has_side_effects=True, vmem_limit_bytes=58 << 20),
+        compiler_params=pltpu.CompilerParams(collective_id=0, has_side_effects=True, vmem_limit_bytes=60 << 20),
         name="brick_convs",
     )(coords, code, feat, cot, kernel)
 
 
-def result_kernel(scale, out_in, dx_in, codes, out, dx, grad, held, rows, bricks, sems):
-    loads = [pltpu.make_async_copy(codes.at[p], held.at[p], sems.at[2 + p]) for p in range(PARTS)]
-    passed = [(out_in, out), (dx_in, dx)]
-    fetches = [pltpu.make_async_copy(src, bricks.at[k], sems.at[k]) for k, (src, _) in enumerate(passed)]
-    copies = [pltpu.make_async_copy(bricks.at[k], dst, sems.at[k]) for k, (_, dst) in enumerate(passed)]
-    for load in loads + fetches:
-        load.start()
+def result_kernel(scale, out_in, dx_in, codes, out, dx, grad, rows, sems):
+    copies = [pltpu.make_async_copy(out_in, out, sems.at[0]), pltpu.make_async_copy(dx_in, dx, sems.at[1])]
+    for copy in copies:
+        copy.start()
     half = PART_TAPS * C // 2
     stores = []
     for part in range(PARTS):
-        if part >= 2:
-            fetches[part - 2].wait()
-            copies[part - 2].start()
-        loads[part].wait()
         for core in range(2):
 
-            @pl.loop(0, GROUP // 4)
-            def _(four):
-                blocks = [decode(held[part, core, 4 * four + n])[:CHUNK] for n in range(4)]
-                start = pl.multiple_of(core * half + four * 4 * CHUNK, 8)
-                rows[part, pl.ds(start, 4 * CHUNK)] = jnp.concatenate(blocks, axis=0) * scale
+            @pl.loop(0, GROUP // 8)
+            def _(eight):
+                blocks = decode(codes[part, core, pl.ds(eight * 8, 8)]) * scale
+                start = pl.multiple_of(core * half + eight * 8 * CHUNK, 8)
+                rows[part, pl.ds(start, 8 * CHUNK)] = jnp.concatenate([blocks[n, :CHUNK] for n in range(8)], axis=0)
 
         first = 0
         taps = ORDER[part]
@@ -449,7 +428,7 @@
                 store = pltpu.make_async_copy(
                     rows.at[part, pl.ds(first * C, (n - first) * C)],
                     grad.at[pl.ds(taps[first] * C, (n - first) * C)],
-                    sems.at[2 + PARTS + len(stores)],
+                    sems.at[2 + len(stores)],
                 )
                 store.start()
                 stores.append(store)
@@ -459,7 +438,7 @@
 
 
 def results(out, dx, codes, scale):
-    anywhere = pl.BlockSpec(memory_space=pl.ANY)
+    anywhere, vmem = pl.BlockSpec(memory_space=pl.ANY), pl.BlockSpec(memory_space=pltpu.VMEM)
     return pl.pallas_call(
         functools.partial(result_kernel, scale),
         out_shape=[
@@ -467,15 +446,13 @@
             jax.ShapeDtypeStruct((SLOTS, 8, 64, C), BF),
             jax.ShapeDtypeStruct((TAPS * C, C), F32),
         ],
-        in_specs=[anywhere] * 3,
+        in_specs=[vmem] * 3,
         out_specs=[anywhere] * 3,
         scratch_shapes=[
-            pltpu.VMEM((PARTS, 2, GROUP, ROWS, C), jnp.int16),
             pltpu.VMEM((PARTS, PART_TAPS * C, C), F32),
-            pltpu.VMEM((2, SLOTS, 8, 64, C), BF),
             pltpu.SemaphoreType.DMA((2 + 4 * PARTS,)),
         ],
-        compiler_params=pltpu.CompilerParams(vmem_limit_bytes=58 << 20),
+        compiler_params=pltpu.CompilerParams(vmem_limit_bytes=48 << 20),
         name="results",
     )(out, dx, codes)
 

time: 55.7 us -> 51.8 us (0.930)
  Pallas kernels: 54.3 us -> 50.4 us
    pallas_call x1, Pallas kernels: 51.2 us -> 48.7 us  [main_call(): pl.pallas_call(main_kernel, out_shape=[pltpu.VMEM((SLOTS, 8, 64, C), BF),...]
    pallas_call x1, Pallas kernels: 3.03 us -> 1.71 us  [results(): pl.pallas_call(functools.partial(result_kernel, scale), out_shape=[jax.Sh...]
where the time goes in v3:
time: 51.8 us; the launch traced here: 51.7 us
  Pallas kernels  50.4 us (97%)
  between operations  1.29 us (2%)
    pallas_call x1, Pallas kernels, main_call(): pl.pallas_call(main_kernel, out_shape=[pltpu.VMEM((SLOTS, 8, 64, C), BF),...  48.7 us
    pallas_call x1, Pallas kernels, results(): pl.pallas_call(functools.partial(result_kernel, scale), out_shape=[jax.Sh...  1.71 us

profile of v3, /device:TPU:1, one launch (start us, length us, event | category | flops | bytes accessed | tf_op | source)
XLA Modules:
  0.0 51.7 jit_solution(1738615898120770329)
XLA Ops:
  1.3 48.7 %brick_convs.1 = (bf16[4,8,64,128]{3,2,1,0:T(8,128)(2,1)S(1)}, bf16[4,8,64,128]{3,2,1,0:T(8,128)(2,1)S(1)}, s16[4,2,32,16,128]{4,3,2,1,0:T(8,128)(2,1)S(1)}) custom-call(s32[1,4]{1,0:T(1,128)} %coords.1, s32[1]{0:T(128)S(6)} %copy.8.code, bf16[4,8,64,128]{3,2,1,0:T(8,128)(2,1)} %bitcast.4, bf16[4,8,64,128]{3,2,1,0:T(8,128)(2,1)} %bitcast.5, ...), custom_call_target="tpu_custom_call" | custom-call | tf_op jit(solution)/shard_map/brick_convs/pallas_call | solution.py:386
  50.0 1.7 %results.1 = (bf16[4,8,64,128]{3,2,1,0:T(8,128)(2,1)}, bf16[4,8,64,128]{3,2,1,0:T(8,128)(2,1)}, f32[3456,128]{1,0:T(8,128)}) custom-call(bf16[4,8,64,128]{3,2,1,0:T(8,128)(2,1)S(1)} %get-tuple-element.9.out_in, bf16[4,8,64,128]{3,2,1,0:T(8,128)(2,1)S(1)} %get-tuple-element.10.dx_in, s16[4,2,32,16,128]{4,3,2,1,0:T(8,128)(2,1)S(1)} %get-tuple-element.11.codes), custom_call_target="tpu_custom_call" | custom-call | tf_op jit(solution)/shard_map/results/pallas_call | solution.py:442

commit v4 on v3

--- a/solution.py
+++ b/solution.py
@@ -39,18 +39,24 @@
     )
 
 
-def neighbours(slab_coord, pos):
+def around(pos):
     row, col = pos >> 2, pos & 3
+    inside_y = {-1: row > 0, 0: pos < 16, 1: row < 3}
+    inside_x = {-1: col > 0, 0: pos < 16, 1: col < 3}
+    return {
+        (dy, dx): jnp.where(inside_y[dy] & inside_x[dx] & (pos < 16), pos + 4 * dy + dx, 99)
+        for dy in (-1, 0, 1)
+        for dx in (-1, 0, 1)
+    }
+
+
+def slots_of(wanted, coord):
     slots = {}
-    for dy in (-1, 0, 1):
-        for dx in (-1, 0, 1):
-            y, x = row + dy, col + dx
-            inside = (y >= 0) & (y < 4) & (x >= 0) & (x < 4) & (pos < 16)
-            wanted = jnp.where(inside, y * 4 + x, 99)
-            slot = jnp.int32(SLOTS)
-            for k in range(SLOTS):
-                slot = jnp.where(slab_coord(k) == wanted, k, slot)
-            slots[dy, dx] = slot
+    for offset, position in wanted.items():
+        slot = jnp.int32(SLOTS)
+        for k in range(SLOTS):
+            slot = jnp.where(coord[k] == position, k, slot)
+        slots[offset] = slot
     return slots
 
 
@@ -115,8 +121,8 @@
     near_y, near_z = [(y + step) & 7 for step in range(8)], [(z + step) & 7 for step in range(8)]
 
     def team(kind):
-        for step_x in range(4):
-            for step in range(8):
+        for step in (4, 3, 5, 2, 6, 1, 7, 0):
+            for step_x in (2, 1, 3, 0):
                 if step_x or step:
                     row, column = near_x[step_x], (near_y, near_z)[kind][step]
                     where = device(z, row, core, column) if kind == 0 else device(column, row, core, y)
@@ -125,21 +131,6 @@
     def ring(kind):
         for step in range(1, 8):
             yield device(near_z[step], x, core, y) if kind == 0 else device(z, x, core, near_y[step])
-
-    barrier = pltpu.get_barrier_semaphore()
-    pl.semaphore_signal(barrier, inc=1, device_id=other, device_id_type=MESH)
-
-    @pl.when(has_upper & (core == 1))
-    def _():
-        pl.semaphore_signal(barrier, inc=1, device_id=upper, device_id_type=MESH)
-
-    @pl.when(has_lower & (core == 0))
-    def _():
-        pl.semaphore_signal(barrier, inc=1, device_id=lower, device_id_type=MESH)
-
-    for kind in range(2):
-        for _, peer in team(kind):
-            pl.semaphore_signal(barrier, inc=1, device_id=peer, device_id_type=MESH)
 
     loads = [
         pltpu.make_async_copy(feat, V.at[pl.ds(0, SLOTS)], load_sem.at[0]),
@@ -148,6 +139,21 @@
     ]
     for load in loads:
         load.start()
+    barrier = pltpu.get_barrier_semaphore()
+    pl.semaphore_signal(barrier, inc=1, device_id=other, device_id_type=MESH)
+
+    @pl.when(has_upper & (core == 1))
+    def _():
+        pl.semaphore_signal(barrier, inc=1, device_id=upper, device_id_type=MESH)
+
+    @pl.when(has_lower & (core == 0))
+    def _():
+        pl.semaphore_signal(barrier, inc=1, device_id=lower, device_id_type=MESH)
+
+    for kind in range(2):
+        for _, peer in team(kind):
+            pl.semaphore_signal(barrier, inc=1, device_id=peer, device_id_type=MESH)
+
     for cells in (V, U):
         cells[SLOTS] = jnp.zeros((8, 64, C), BF)
     for planes in (HV, HU):
@@ -169,19 +175,24 @@
         return tap + flip_z * (18 - 18 * tz) + flip_y * (6 - 6 * ty) + flip_x * (2 - 2 * tx)
 
     def inner(cells, even, odd):
+        own = [coords[0, k] for k in range(SLOTS)]
+
         @pl.loop(0, SLOTS)
         def _(i):
-            slots = neighbours(lambda k: coords[0, k], coords[0, i])
+            slots = slots_of(around(coords[0, i]), own)
 
             @pl.loop(0, 8)
             def _(plane):
                 build_plane(lambda j, a, n: cells[j, plane, pl.ds(a, n), :], slots, even, odd, i, plane + 1)
 
     def outer(planes, even, odd):
+        sides = [[jnp.where(there, near[d, 0, k], 16) for k in range(SLOTS)] for d, there in ((0, has_lower), (1, has_upper))]
+
         @pl.loop(0, SLOTS)
         def _(i):
-            for d, plane, there in ((0, 0, has_lower), (1, 9, has_upper)):
-                slots = neighbours(lambda k: jnp.where(there, near[d, 0, k], 16), coords[0, i])
+            wanted = around(coords[0, i])
+            for d, plane in ((0, 0), (1, 9)):
+                slots = slots_of(wanted, sides[d])
                 build_plane(lambda j, a, n: planes[d, j, pl.ds(a, n), :], slots, even, odd, i, plane)
 
     loads[0].wait()
@@ -206,11 +217,12 @@
         for n, t in enumerate(ORDER[part]):
             grad[part, n * C : (n + 1) * C] = terms[mirrored(t)]
 
-    for t, term in products(MIDDLE + LOW + HIGH, cot_t[...], lambda t: shifted(even_v, odd_v, t)):
-        terms[t] = term
+    def own_terms(taps):
+        for t, term in products(taps, cot_t[...], lambda t: shifted(even_v, odd_v, t)):
+            terms[t] = term
+
+    own_terms(MIDDLE)
     fill(0)
-    for n in range(len(ORDER[PARTS - 1]), PART_TAPS):
-        grad[PARTS - 1, n * C : (n + 1) * C] = jnp.zeros((C, C), F32)
 
     half = PART_TAPS * C // 2
 
@@ -218,7 +230,6 @@
         src = grad.at[part, pl.ds(pl.multiple_of((1 - core) * half, 8), half)]
         return remote(src, sibling.at[part, pl.ds(0, half)], core_send.at[part], core_recv.at[part], other)
 
-    inner(U, even_u, odd_u)
     pl.semaphore_wait(barrier, 2 * GROUP - 1 + ((has_upper & (core == 1)) | (has_lower & (core == 0))).astype(jnp.int32))
 
     halos = []
@@ -261,7 +272,11 @@
 
         scatter(part)
 
+    own_terms(LOW + HIGH)
+    for n in range(len(ORDER[PARTS - 1]), PART_TAPS):
+        grad[PARTS - 1, n * C : (n + 1) * C] = jnp.zeros((C, C), F32)
     send_part(0)
+    inner(U, even_u, odd_u)
 
     end_halo(0)
     near_copy = pltpu.make_async_copy(HC, near, load_sem.at[3])
@@ -334,7 +349,7 @@
 
         exchange(part)
 
-    @pl.loop(0, 2)
+    @pl.loop(0, 1)
     def _(i):
         dx[i] = convolve(i, True)
 
@@ -351,7 +366,7 @@
 
         publish(part)
 
-    @pl.loop(2, SLOTS)
+    @pl.loop(1, SLOTS)
     def _(i):
         dx[i] = convolve(i, True)
 

time: 51.8 us -> 49.7 us (0.959)
  Pallas kernels: 50.4 us -> 48.2 us
    pallas_call x1, Pallas kernels: 48.7 us -> 46.5 us  [main_call(): pl.pallas_call(main_kernel, out_shape=[pltpu.VMEM((SLOTS, 8, 64, C), BF),...]
where the time goes in v4:
time: 49.7 us; the launch traced here: 49.5 us
  Pallas kernels  48.2 us (97%)
  between operations  1.29 us (3%)
    pallas_call x1, Pallas kernels, main_call(): pl.pallas_call(main_kernel, out_shape=[pltpu.VMEM((SLOTS, 8, 64, C), BF),...  46.5 us
    pallas_call x1, Pallas kernels, results(): pl.pallas_call(functools.partial(result_kernel, scale), out_shape=[jax.Sh...  1.71 us

profile of v4, /device:TPU:1, one launch (start us, length us, event | category | flops | bytes accessed | tf_op | source)
XLA Modules:
  0.0 49.5 jit_solution(78262208205405770)
XLA Ops:
  1.3 46.5 %brick_convs.1 = (bf16[4,8,64,128]{3,2,1,0:T(8,128)(2,1)S(1)}, bf16[4,8,64,128]{3,2,1,0:T(8,128)(2,1)S(1)}, s16[4,2,32,16,128]{4,3,2,1,0:T(8,128)(2,1)S(1)}) custom-call(s32[1,4]{1,0:T(1,128)} %coords.1, s32[1]{0:T(128)S(6)} %copy.8.code, bf16[4,8,64,128]{3,2,1,0:T(8,128)(2,1)} %bitcast.4, bf16[4,8,64,128]{3,2,1,0:T(8,128)(2,1)} %bitcast.5, ...), custom_call_target="tpu_custom_call" | custom-call | tf_op jit(solution)/shard_map/brick_convs/pallas_call | solution.py:401
  47.8 1.7 %results.1 = (bf16[4,8,64,128]{3,2,1,0:T(8,128)(2,1)}, bf16[4,8,64,128]{3,2,1,0:T(8,128)(2,1)}, f32[3456,128]{1,0:T(8,128)}) custom-call(bf16[4,8,64,128]{3,2,1,0:T(8,128)(2,1)S(1)} %get-tuple-element.9.out_in, bf16[4,8,64,128]{3,2,1,0:T(8,128)(2,1)S(1)} %get-tuple-element.10.dx_in, s16[4,2,32,16,128]{4,3,2,1,0:T(8,128)(2,1)S(1)} %get-tuple-element.11.codes), custom_call_target="tpu_custom_call" | custom-call | tf_op jit(solution)/shard_map/results/pallas_call | solution.py:457

commit v5 on v4

--- a/solution.py
+++ b/solution.py
@@ -103,8 +103,8 @@
 
 
 def main_kernel(
-    coords, code, feat, cot, kernel, out, dx, gathered,
-    V, U, HV, HU, HC, mine_c, near, KV, even_v, odd_v, even_u, odd_u, cot_t, edge_t, terms, grad, sibling,
+    coords_in, code_in, feat, cot, kernel, out, dx, gathered,
+    coords, code, V, U, HV, HU, HC, mine_c, near, KV, even_v, odd_v, even_u, odd_u, cot_t, edge_t, terms, grad, sibling,
     out_codes, in_codes, mid_codes, mid_in,
     load_sem, halo_send, halo_recv, core_send, core_recv, s1, r1, s2, r2, s3, r3, hand_send, hand_recv,
 ):
@@ -137,7 +137,8 @@
         pltpu.make_async_copy(cot, U.at[pl.ds(0, SLOTS)], load_sem.at[1]),
         pltpu.make_async_copy(kernel, KV, load_sem.at[2]),
     ]
-    for load in loads:
+    codes = [pltpu.make_async_copy(coords_in, coords, load_sem.at[4]), pltpu.make_async_copy(code_in, code, load_sem.at[5])]
+    for load in codes + loads:
         load.start()
     barrier = pltpu.get_barrier_semaphore()
     pl.semaphore_signal(barrier, inc=1, device_id=other, device_id_type=MESH)
@@ -162,6 +163,8 @@
     for z0 in (0, 9):
         even_v[:, :, z0] = jnp.zeros((3, SLOTS, 64, C), BF)
         odd_v[:, :, z0] = jnp.zeros((3, SLOTS, 80, C), BF)
+    for copy in codes:
+        copy.wait()
     lane = lax.broadcasted_iota(jnp.int32, (8, C), 1)
     row = jnp.full((8, C), 16, jnp.int32)
     for k in range(SLOTS):
@@ -236,8 +239,8 @@
     for d, (there, peer, plane) in enumerate(((has_upper, upper, 7), (has_lower, lower, 0))):
         group = [
             remote(mine_c, HC.at[d], halo_send.at[d, 0], halo_recv.at[d, 0], peer),
-            remote(feat.at[:, plane], HV.at[d, pl.ds(0, SLOTS)], halo_send.at[d, 1], halo_recv.at[d, 1], peer),
-            remote(cot.at[:, plane], HU.at[d, pl.ds(0, SLOTS)], halo_send.at[d, 2], halo_recv.at[d, 2], peer),
+            remote(V.at[pl.ds(0, SLOTS), plane], HV.at[d, pl.ds(0, SLOTS)], halo_send.at[d, 1], halo_recv.at[d, 1], peer),
+            remote(U.at[pl.ds(0, SLOTS), plane], HU.at[d, pl.ds(0, SLOTS)], halo_send.at[d, 2], halo_recv.at[d, 2], peer),
         ]
         halos.append((there, group))
 
@@ -392,7 +395,7 @@
 
 
 def main_call(coords, code, feat, cot, kernel):
-    smem, vmem = pl.BlockSpec(memory_space=pltpu.SMEM), pl.BlockSpec(memory_space=pltpu.VMEM)
+    vmem = pl.BlockSpec(memory_space=pltpu.VMEM)
     anywhere = pl.BlockSpec(memory_space=pl.ANY)
     dma = pltpu.SemaphoreType.DMA
     cells, planes = pltpu.VMEM((SLOTS + 1, 8, 64, C), BF), pltpu.VMEM((2, SLOTS + 1, 64, C), BF)
@@ -405,15 +408,15 @@
             pltpu.VMEM((SLOTS, 8, 64, C), BF),
             pltpu.VMEM((PARTS, 2, GROUP, ROWS, C), jnp.int16),
         ],
-        in_specs=[smem] * 2 + [anywhere] * 3,
+        in_specs=[anywhere] * 5,
         out_specs=[vmem] * 3,
         scratch_shapes=[
-            cells, cells, planes, planes, pltpu.VMEM((2, 8, C), jnp.int32), pltpu.VMEM((8, C), jnp.int32),
+            pltpu.SMEM((1, SLOTS), jnp.int32), pltpu.SMEM((1,), jnp.int32), cells, cells, planes, planes, pltpu.VMEM((2, 8, C), jnp.int32), pltpu.VMEM((8, C), jnp.int32),
             pltpu.SMEM((2, 8, C), jnp.int32), pltpu.VMEM((TAPS, C, C), BF), even, odd, even, odd,
             pltpu.VMEM((C, SLOTS * CELLS), BF), pltpu.VMEM((2, C, SLOTS * 64), BF), pltpu.VMEM((TAPS, C, C), F32),
             pltpu.VMEM((PARTS, PART_TAPS * C + 8, C), F32), pltpu.VMEM((PARTS, PART_TAPS * C // 2 + 8, C), F32),
             codes, codes, pltpu.VMEM((PARTS, ROWS, C), jnp.int16), pltpu.VMEM((PARTS, 8, ROWS, C), jnp.int16),
-            dma((4,)), dma((2, 3)), dma((2, 3)), dma((PARTS,)), dma((PARTS,)), dma((PARTS,)), dma((PARTS,)),
+            dma((6,)), dma((2, 3)), dma((2, 3)), dma((PARTS,)), dma((PARTS,)), dma((PARTS,)), dma((PARTS,)),
             dma((PARTS,)), dma((PARTS,)), dma((PARTS,)), dma((PARTS,)), dma((PARTS,)), dma((PARTS,)),
         ],
         compiler_params=pltpu.CompilerParams(collective_id=0, has_side_effects=True, vmem_limit_bytes=60 << 20),

time: 49.7 us -> 49.5 us (level)
  no operation moved by 1% of the time
where the time goes in v5:
time: 49.5 us; the launch traced here: 49.4 us
  Pallas kernels  48.1 us (97%)
  between operations  1.29 us (3%)
    pallas_call x1, Pallas kernels, main_call(): pl.pallas_call(main_kernel, out_shape=[pltpu.VMEM((SLOTS, 8, 64, C), BF),...  46.4 us
    pallas_call x1, Pallas kernels, results(): pl.pallas_call(functools.partial(result_kernel, scale), out_shape=[jax.Sh...  1.71 us

profile of v5, /device:TPU:1, one launch (start us, length us, event | category | flops | bytes accessed | tf_op | source)
XLA Modules:
  0.0 49.4 jit_solution(7551309849195208735)
XLA Ops:
  1.3 46.4 %brick_convs.1 = (bf16[4,8,64,128]{3,2,1,0:T(8,128)(2,1)S(1)}, bf16[4,8,64,128]{3,2,1,0:T(8,128)(2,1)S(1)}, s16[4,2,32,16,128]{4,3,2,1,0:T(8,128)(2,1)S(1)}) custom-call(s32[1,4]{1,0:T(1,128)} %coords_in.1, s32[1]{0:T(128)S(6)} %copy.8.code_in, bf16[4,8,64,128]{3,2,1,0:T(8,128)(2,1)} %bitcast.4, bf16[4,8,64,128]{3,2,1,0:T(8,128)(2,1)} %bitcast.5, ...), custom_call_target="tpu_custom_call" | custom-call | tf_op jit(solution)/shard_map/brick_convs/pallas_call | solution.py:404
  47.7 1.7 %results.1 = (bf16[4,8,64,128]{3,2,1,0:T(8,128)(2,1)}, bf16[4,8,64,128]{3,2,1,0:T(8,128)(2,1)}, f32[3456,128]{1,0:T(8,128)}) custom-call(bf16[4,8,64,128]{3,2,1,0:T(8,128)(2,1)S(1)} %get-tuple-element.9.out_in, bf16[4,8,64,128]{3,2,1,0:T(8,128)(2,1)S(1)} %get-tuple-element.10.dx_in, s16[4,2,32,16,128]{4,3,2,1,0:T(8,128)(2,1)S(1)} %get-tuple-element.11.codes), custom_call_target="tpu_custom_call" | custom-call | tf_op jit(solution)/shard_map/results/pallas_call | solution.py:460

commit v6 on v5

--- a/solution.py
+++ b/solution.py
@@ -104,7 +104,7 @@
 
 def main_kernel(
     coords_in, code_in, feat, cot, kernel, out, dx, gathered,
-    coords, code, V, U, HV, HU, HC, mine_c, near, KV, even_v, odd_v, even_u, odd_u, cot_t, edge_t, terms, grad, sibling,
+    coords, code, V, U, HVS, HVO, HU, HCS, HCO, mine_c, near, KV, even_v, odd_v, even_u, odd_u, cot_t, edge_t, terms, grad, sibling,
     out_codes, in_codes, mid_codes, mid_in,
     load_sem, halo_send, halo_recv, core_send, core_recv, s1, r1, s2, r2, s3, r3, hand_send, hand_recv,
 ):
@@ -157,9 +157,8 @@
 
     for cells in (V, U):
         cells[SLOTS] = jnp.zeros((8, 64, C), BF)
-    for planes in (HV, HU):
-        for d in range(2):
-            planes[d, SLOTS] = jnp.zeros((64, C), BF)
+    for planes in (HVS, HVO, HU.at[0], HU.at[1]):
+        planes[SLOTS] = jnp.zeros((64, C), BF)
     for z0 in (0, 9):
         even_v[:, :, z0] = jnp.zeros((3, SLOTS, 64, C), BF)
         odd_v[:, :, z0] = jnp.zeros((3, SLOTS, 80, C), BF)
@@ -170,6 +169,9 @@
     for k in range(SLOTS):
         row = jnp.where(lane == k, coords[0, k], row)
     mine_c[...] = row
+    for d in range(2):
+        for k in range(SLOTS):
+            near[d, 0, k] = 16
     flip_code = code[0]
     flip_x, flip_y, flip_z = flip_code & 1, (flip_code >> 1) & 1, (flip_code >> 2) & 1
 
@@ -188,15 +190,13 @@
             def _(plane):
                 build_plane(lambda j, a, n: cells[j, plane, pl.ds(a, n), :], slots, even, odd, i, plane + 1)
 
-    def outer(planes, even, odd):
-        sides = [[jnp.where(there, near[d, 0, k], 16) for k in range(SLOTS)] for d, there in ((0, has_lower), (1, has_upper))]
+    def outer(planes, even, odd, n, d, there):
+        theirs = [jnp.where(there, near[n, 0, k], 16) for k in range(SLOTS)]
 
         @pl.loop(0, SLOTS)
         def _(i):
-            wanted = around(coords[0, i])
-            for d, plane in ((0, 0), (1, 9)):
-                slots = slots_of(wanted, sides[d])
-                build_plane(lambda j, a, n: planes[d, j, pl.ds(a, n), :], slots, even, odd, i, plane)
+            slots = slots_of(around(coords[0, i]), theirs)
+            build_plane(lambda j, a, m: planes[j, pl.ds(a, m), :], slots, even, odd, i, 9 * d)
 
     loads[0].wait()
     inner(V, even_v, odd_v)
@@ -235,22 +235,21 @@
 
     pl.semaphore_wait(barrier, 2 * GROUP - 1 + ((has_upper & (core == 1)) | (has_lower & (core == 0))).astype(jnp.int32))
 
+    has_outer = jnp.where(core == 0, has_lower, has_upper)
+    beyond = {"slab": lax.rem(slab + 63 + 2 * core, 64)}
     halos = []
-    for d, (there, peer, plane) in enumerate(((has_upper, upper, 7), (has_lower, lower, 0))):
-        group = [
-            remote(mine_c, HC.at[d], halo_send.at[d, 0], halo_recv.at[d, 0], peer),
-            remote(V.at[pl.ds(0, SLOTS), plane], HV.at[d, pl.ds(0, SLOTS)], halo_send.at[d, 1], halo_recv.at[d, 1], peer),
-            remote(U.at[pl.ds(0, SLOTS), plane], HU.at[d, pl.ds(0, SLOTS)], halo_send.at[d, 2], halo_recv.at[d, 2], peer),
-        ]
-        halos.append((there, group))
+    for n, (peer, plane, c_land, v_land) in enumerate(((other, 7 * (1 - core), HCS, HVS), (beyond, 7 * core, HCO, HVO))):
+        halos.append(
+            [
+                remote(mine_c, c_land, halo_send.at[n, 0], halo_recv.at[n, 0], peer),
+                remote(V.at[pl.ds(0, SLOTS), plane], v_land.at[pl.ds(0, SLOTS)], halo_send.at[n, 1], halo_recv.at[n, 1], peer),
+                remote(U.at[pl.ds(0, SLOTS), plane], HU.at[n, pl.ds(0, SLOTS)], halo_send.at[n, 2], halo_recv.at[n, 2], peer),
+            ]
+        )
 
     def start_halo(k):
-        for there, group in halos:
-            pl.when(there)(group[k].start)
-
-    def end_halo(k):
-        for (there, _), (_, group) in zip(reversed(halos), halos, strict=True):
-            pl.when(there)(group[k].wait_recv)
+        pl.when(has_outer)(halos[1][k].start)
+        halos[0][k].start()
 
     start_halo(0)
     start_halo(1)
@@ -281,22 +280,29 @@
     send_part(0)
     inner(U, even_u, odd_u)
 
-    end_halo(0)
-    near_copy = pltpu.make_async_copy(HC, near, load_sem.at[3])
-    near_copy.start()
-    end_halo(1)
-    near_copy.wait()
-    outer(HV, even_v, odd_v)
-
-    def edge_cells(t):
-        ty, tx, side = t // 3 % 3, t % 3, 9 * (t // 18)
-        if ty == 1:
-            return even_v[tx, :, side].reshape(SLOTS * 64, C)
-        return odd_v[tx, :, side, 8 * ty : 8 * ty + 64].reshape(SLOTS * 64, C)
-
-    for d, taps in enumerate((LOW, HIGH)):
-        for t, term in products(taps, edge_t[d], edge_cells):
-            terms[t] += term
+    for n, (d, there) in enumerate(((1 - core, True), (core, has_outer))):
+        near_copy = pltpu.make_async_copy((HCS, HCO)[n], near.at[n], load_sem.at[3])
+
+        def arrived(n=n, near_copy=near_copy):
+            halos[n][0].wait_recv()
+            near_copy.start()
+            halos[n][1].wait_recv()
+            near_copy.wait()
+
+        if n == 0:
+            arrived()
+        else:
+            pl.when(there)(arrived)
+        outer((HVS, HVO)[n], even_v, odd_v, n, d, there)
+
+        def edge_cells(t, d=d):
+            ty, tx = t // 3, t % 3
+            if ty == 1:
+                return even_v[tx, :, 9 * d].reshape(SLOTS * 64, C)
+            return odd_v[tx, :, 9 * d, 8 * ty : 8 * ty + 64].reshape(SLOTS * 64, C)
+
+        for t, term in products(LOW, edge_t[d], edge_cells):
+            terms[t + 18 * d] += term
     for part in range(1, PARTS):
         fill(part)
         to_core(part).start()
@@ -324,8 +330,10 @@
     def _(i):
         out[i] = convolve(i, False)
 
-    end_halo(2)
-    outer(HU, even_u, odd_u)
+    halos[0][2].wait_recv()
+    pl.when(has_outer)(halos[1][2].wait_recv)
+    outer(HU.at[0], even_u, odd_u, 0, 1 - core, True)
+    outer(HU.at[1], even_u, odd_u, 1, core, has_outer)
 
     def exchange(part):
         landing = mid_in.at[part, ring_me[part % 2]]
@@ -387,9 +395,10 @@
         several(mid_in.at[part], 7, s2.at[part], r2.at[part]).wait_send()
         several(gathered.at[part, core], GROUP - 1, s3.at[part], r3.at[part]).wait_send()
         hand(part).wait_send()
-    for there, group in halos:
-        for copy in group:
-            pl.when(there)(copy.wait_send)
+    for copy in halos[0]:
+        copy.wait_send()
+    for copy in halos[1]:
+        pl.when(has_outer)(copy.wait_send)
     for part in range(PARTS):
         hand(part).wait_recv()
 
@@ -399,6 +408,7 @@
     anywhere = pl.BlockSpec(memory_space=pl.ANY)
     dma = pltpu.SemaphoreType.DMA
     cells, planes = pltpu.VMEM((SLOTS + 1, 8, 64, C), BF), pltpu.VMEM((2, SLOTS + 1, 64, C), BF)
+    side, row = pltpu.VMEM((SLOTS + 1, 64, C), BF), pltpu.VMEM((8, C), jnp.int32)
     even, odd = pltpu.VMEM((3, SLOTS, 10, 64, C), BF), pltpu.VMEM((3, SLOTS, 10, 80, C), BF)
     codes = pltpu.VMEM((PARTS, GROUP, ROWS, C), jnp.int16)
     return pl.pallas_call(
@@ -411,7 +421,7 @@
         in_specs=[anywhere] * 5,
         out_specs=[vmem] * 3,
         scratch_shapes=[
-            pltpu.SMEM((1, SLOTS), jnp.int32), pltpu.SMEM((1,), jnp.int32), cells, cells, planes, planes, pltpu.VMEM((2, 8, C), jnp.int32), pltpu.VMEM((8, C), jnp.int32),
+            pltpu.SMEM((1, SLOTS), jnp.int32), pltpu.SMEM((1,), jnp.int32), cells, cells, side, side, planes, row, row, row,
             pltpu.SMEM((2, 8, C), jnp.int32), pltpu.VMEM((TAPS, C, C), BF), even, odd, even, odd,
             pltpu.VMEM((C, SLOTS * CELLS), BF), pltpu.VMEM((2, C, SLOTS * 64), BF), pltpu.VMEM((TAPS, C, C), F32),
             pltpu.VMEM((PARTS, PART_TAPS * C + 8, C), F32), pltpu.VMEM((PARTS, PART_TAPS * C // 2 + 8, C), F32),

time: 49.5 us -> 50.2 us (1.014)
  Pallas kernels: 48.1 us -> 48.8 us
    pallas_call x1, Pallas kernels: 46.4 us -> 47.1 us  [main_call(): pl.pallas_call(main_kernel, out_shape=[pltpu.VMEM((SLOTS, 8, 64, C), BF),...]
where the time goes in v6:
time: 50.2 us; the launch traced here: 50.1 us
  Pallas kernels  48.8 us (97%)
  between operations  1.29 us (3%)
    pallas_call x1, Pallas kernels, main_call(): pl.pallas_call(main_kernel, out_shape=[pltpu.VMEM((SLOTS, 8, 64, C), BF),...  47.1 us
    pallas_call x1, Pallas kernels, results(): pl.pallas_call(functools.partial(result_kernel, scale), out_shape=[jax.Sh...  1.71 us

profile of v6, /device:TPU:1, one launch (start us, length us, event | category | flops | bytes accessed | tf_op | source)
XLA Modules:
  0.0 50.1 jit_solution(14896797371830152458)
XLA Ops:
  1.3 47.1 %brick_convs.1 = (bf16[4,8,64,128]{3,2,1,0:T(8,128)(2,1)S(1)}, bf16[4,8,64,128]{3,2,1,0:T(8,128)(2,1)S(1)}, s16[4,2,32,16,128]{4,3,2,1,0:T(8,128)(2,1)S(1)}) custom-call(s32[1,4]{1,0:T(1,128)} %coords_in.1, s32[1]{0:T(128)S(6)} %copy.8.code_in, bf16[4,8,64,128]{3,2,1,0:T(8,128)(2,1)} %bitcast.4, bf16[4,8,64,128]{3,2,1,0:T(8,128)(2,1)} %bitcast.5, ...), custom_call_target="tpu_custom_call" | custom-call | tf_op jit(solution)/shard_map/brick_convs/pallas_call | solution.py:414
  48.4 1.7 %results.1 = (bf16[4,8,64,128]{3,2,1,0:T(8,128)(2,1)}, bf16[4,8,64,128]{3,2,1,0:T(8,128)(2,1)}, f32[3456,128]{1,0:T(8,128)}) custom-call(bf16[4,8,64,128]{3,2,1,0:T(8,128)(2,1)S(1)} %get-tuple-element.9.out_in, bf16[4,8,64,128]{3,2,1,0:T(8,128)(2,1)S(1)} %get-tuple-element.10.dx_in, s16[4,2,32,16,128]{4,3,2,1,0:T(8,128)(2,1)S(1)} %get-tuple-element.11.codes), custom_call_target="tpu_custom_call" | custom-call | tf_op jit(solution)/shard_map/results/pallas_call | solution.py:470
